TPU v7x, 32 devices: a whole 2x2x4 slice. The times are simulated.
32 devices in a mesh: front: 8 (over z, y), sect: 4 (over x, core).
Axes of the slice: x: 2, y: 2, z: 4, core: 2. Of those that a mesh axis runs over, the one named last changes fastest.
Arguments:
- pivot_rows: float32 [8, 4, 512, 512], P('front', 'sect'), may hold values from -6 to 6
- sections: float32 [8, 4, 4, 256, 512], P('front', 'sect'), may hold values from -6 to 6
- sect_vectors: bfloat16 [8, 4, 4, 256, 512], P('front', 'sect'), may hold values from -0.375 to 0.375
- sect_factors: bfloat16 [8, 4, 4, 512, 512], P('front', 'sect'), may hold values from -0.125 to 0.125
- routes: int32 [8, 4, 1024, 1], P('front', 'sect'), may hold values from 0 to 7; in each aligned block of 1024 rows (0 to 1023, 1024 to 2047, ..., all dimensions but the last counted through in order) at most 192 rows name the same one
- parent_vectors: bfloat16 [8, 4, 1536, 512], P('front', 'sect'), may hold values from -0.078125 to 0.078125
- parent_factor: bfloat16 [8, 512, 512], P('front'), may hold values from -0.25 to 0.25
Outputs:
- top_rows: float32 [8, 4, 512, 512], P('front', 'sect')
- parent_rows: float32 [8, 4, 1536, 512], P('front', 'sect')
Inputs may be any that keep to these rules, and one draw needn't show every extreme that they name: `routes`: the rows of one section name each parent owner at most 192 times, a bound that some block reaches.
All inputs are finite; a program needn't handle non-finite values.
Results may differ from a plain program's by a relative error of at most 0.0003.
Values sent between devices are 32-bit elements; how exact they have to be, the bound alone decides.
A program may use at most 128 MiB of HBM per device.

v0:
```python
import jax
import jax.numpy as jnp
from jax import lax
from jax.sharding import PartitionSpec as P

highest = lax.Precision.HIGHEST


def passed_along(value, axis, steps):
    count = lax.axis_size(axis)
    pairs = [(source, (source + steps) % count) for source in range(count)]
    return lax.ppermute(value, axis, pairs)


def reflect(pivot_block, row_block, vectors, factor):
    vectors = vectors.astype(jnp.float32)
    factor = factor.astype(jnp.float32)
    inner_sum = pivot_block + jnp.einsum("rp,rn->pn", vectors, row_block, precision=highest)
    change = jnp.einsum("qp,qn->pn", factor, inner_sum, precision=highest)
    return (pivot_block - change, row_block - jnp.dot(vectors, change, precision=highest))


def local(pivot_rows, sections, sect_vectors, sect_factors, routes, parent_vectors, parent_factor):
    owner_index = lax.axis_index("sect")
    owners_sect = lax.axis_size("sect")
    blocks = sections[0, 0]
    vectors_all = sect_vectors[0, 0]
    factors_all = sect_factors[0, 0]
    own_pivot = pivot_rows[0, 0]
    pivot_block = own_pivot
    for step_id in range(owners_sect):
        panel_id = (owner_index - step_id) % owners_sect
        row_block = lax.dynamic_index_in_dim(blocks, panel_id, 0, keepdims=False)
        vectors = lax.dynamic_index_in_dim(vectors_all, panel_id, 0, keepdims=False)
        factor = lax.dynamic_index_in_dim(factors_all, panel_id, 0, keepdims=False)
        pivot_block, updated = reflect(pivot_block, row_block, vectors, factor)
        blocks = lax.dynamic_update_index_in_dim(blocks, updated, panel_id, 0)
        pivot_block = passed_along(pivot_block, "sect", 1)
    columns = blocks.shape[-1]
    contrib = blocks.reshape(-1, columns)
    row_count = contrib.shape[0]
    owners = lax.axis_size("front")
    capacity = 3 * row_count // (2 * owners)
    destination = routes[0, 0, :, 0]
    onehot = (destination[:, None] == jnp.arange(owners, dtype=jnp.int32)[None, :]).astype(
        jnp.int32
    )
    rank_slot = jnp.sum(jnp.cumsum(onehot, axis=0) * onehot, axis=1) - 1
    slot_index = destination * capacity + rank_slot
    buffer = jnp.zeros((owners * capacity, columns), jnp.float32).at[slot_index].set(contrib)
    buffer = buffer.reshape(owners, capacity, columns)
    arrived = lax.all_to_all(buffer, "front", split_axis=0, concat_axis=0, tiled=True).reshape(
        owners * capacity, columns
    )
    parent_vec = parent_vectors[0, 0].astype(jnp.float32)
    parent_fac = parent_factor[0].astype(jnp.float32)
    partial_value = jnp.einsum("rp,rn->pn", parent_vec, arrived, precision=highest)
    summed = lax.psum(partial_value, "sect")
    change = jnp.einsum("qp,qn->pn", parent_fac, summed, precision=highest)
    result = arrived - jnp.dot(parent_vec, change, precision=highest)
    return (pivot_block[None, None], result[None, None])


def solution(mesh):
    in_specs = (
        P("front", "sect", None, None),
        P("front", "sect", None, None, None),
        P("front", "sect", None, None, None),
        P("front", "sect", None, None, None),
        P("front", "sect", None, None),
        P("front", "sect", None, None),
        P("front", None, None),
    )
    out_specs = (P("front", "sect", None, None), P("front", "sect", None, None))
    return jax.shard_map(local, mesh=mesh, in_specs=in_specs, out_specs=out_specs, check_vma=False)
```

profile of v0, /device:TPU:1, one launch (start us, length us, event | category | flops | bytes accessed | tf_op | source)
XLA Modules:
  0.0 211.5 jit_solution(11890050695604166453)
XLA Ops:
  7.2 0.0 copy-start
  7.2 0.0 copy-start.1
  7.2 2.3 %convolution_add_fusion.3 = f32[512,512]{1,0:T(8,128)S(1)} fusion(f32[1,1,512,512]{3,2,1,0:T(8,128)} %param.7, f32[1,1,4,256,512]{4,3,2,1,0:T(8,128)} %param.8, s32[]{:T(128)S(6)} %select_n.58, bf16[1,1,4,256,512]{4,3,2,1,0:T(8,128)(2,1)} %param.9), kind=kOutput, calls=%fused_computation.13 | convolution fusion | flops 805568512 | bytes 2884608 | tf_op jit(solution)/shard_map/rp,rn->pn/dot_general | solution.py:18
  9.5 0.0 copy-done
  9.5 0.1 copy-done.1
  9.6 2.4 %bitcast_subtract_fusion = (f32[512,512]{1,0:T(8,128)}, f32[512,512]{1,0:T(8,128)}) fusion(f32[1,1,512,512]{3,2,1,0:T(8,128)S(1)} %copy-done.1, f32[512,512]{1,0:T(8,128)S(1)} %convolution_add_fusion.3, bf16[1,1,4,512,512]{4,3,2,1,0:T(8,128)(2,1)S(1)} %copy-done, s32[]{:T(128)S(6)} %select_n.58), kind=kOutput, calls=%fused_computation.26 | convolution fusion | flops 1610874880 | bytes 4718596 | tf_op jit(solution)/shard_map/qp,qn->pn/dot_general | solution.py:19
  12.0 2.6 %collective-permute-start = (f32[512,512]{1,0:T(8,128)}, f32[512,512]{1,0:T(8,128)S(1)}, u32[]{:S(2)}, u32[]{:S(2)}) collective-permute-start(f32[512,512]{1,0:T(8,128)} %get-tuple-element.6), channel_id=1, source_target_pairs={{0,1},{1,2},{2,3},{3,0},{4,5},{5,6},{6,7},{7,4},{8,9},{9,10},{10,1... | collective-permute-start | bytes 3145736 | tf_op jit(solution)/shard_map/ppermute | solution.py:12
  14.6 3.1 %copy.14 = f32[4,256,512]{2,1,0:T(8,128)} copy(f32[4,256,512]{2,1,0:T(8,128)} %bitcast.136) | data formatting | bytes 4194304
  17.7 2.9 %fusion.17 = f32[4,256,512]{2,1,0:T(8,128)} fusion(f32[4,256,512]{2,1,0:T(8,128)} %copy.14, s32[]{:T(128)S(6)} %select_n.58, f32[512,512]{1,0:T(8,128)} %get-tuple-element.7, f32[1,1,4,256,512]{4,3,2,1,0:T(8,128)} %param.8, bf16[1,1,4,256,512]{4,3,2,1,0:T(8,128)(2,1)} %param.9), kind=kOutput, calls=%fused_computation.25 | convolution fusion | flops 805437440 | bytes 2360320 | tf_op jit(solution)/shard_map/dot_general | solution.py:20
  20.6 6.1 %collective-permute-done = f32[512,512]{1,0:T(8,128)S(1)} collective-permute-done((f32[512,512]{1,0:T(8,128)}, f32[512,512]{1,0:T(8,128)S(1)}, u32[]{:S(2)}, u32[]{:S(2)}) %collective-permute-start) | collective-permute-done | bytes 1048608 | tf_op jit(solution)/shard_map/ppermute | solution.py:12
  26.6 1.8 convolution_add_fusion.2
  28.4 0.0 copy-start.5
  28.5 2.4 %fusion.68 = (f32[512,512]{1,0:T(8,128)}, f32[512,512]{1,0:T(8,128)}) fusion(f32[512,512]{1,0:T(8,128)S(1)} %collective-permute-done, f32[512,512]{1,0:T(8,128)S(1)} %convolution_add_fusion.2, bf16[1,1,4,512,512]{4,3,2,1,0:T(8,128)(2,1)S(1)} %copy-done, s32[]{:T(128)S(6)} %select_n.60), kind=kOutput, calls=%fused_computation.88 | convolution fusion | flops 1610874880 | bytes 4718596 | tf_op jit(solution)/shard_map/qp,qn->pn/dot_general | solution.py:19
  30.9 2.4 %collective-permute-start.1 = (f32[512,512]{1,0:T(8,128)}, f32[512,512]{1,0:T(8,128)S(1)}, u32[]{:S(2)}, u32[]{:S(2)}) collective-permute-start(f32[512,512]{1,0:T(8,128)} %get-tuple-element.8), channel_id=1, source_target_pairs={{0,1},{1,2},{2,3},{3,0},{4,5},{5,6},{6,7},{7,4},{8,9},{9,10},{10,1... | collective-permute-start | bytes 3145736 | tf_op jit(solution)/shard_map/ppermute | solution.py:12
  33.3 0.0 copy-done.5
  33.3 2.3 %reduce-window.6 = s32[8,8,128]{2,1,0:T(8,128)S(1)} reduce-window(s32[8,8,128]{2,1,0:T(8,128)S(1)} %fusion.55, s32[]{:T(128)} %constant.91.clone.1), window={size=1x1x128 pad=0_0x0_0x127_0}, to_apply=%region_0.1 | reduce-window | flops 1040384 | bytes 65540 | tf_op jit(solution)/shard_map/reduce-window
  35.5 0.3 slice_reduce_fusion
  35.8 0.2 reduce-window.9
  36.0 1.2 constant_dynamic-slice_fusion.2
  37.2 0.1 add_bitcast_fusion
  37.2 2.8 %fusion.15 = f32[4,256,512]{2,1,0:T(8,128)} fusion(f32[4,256,512]{2,1,0:T(8,128)} %fusion.17, s32[]{:T(128)S(6)} %select_n.60, f32[512,512]{1,0:T(8,128)} %get-tuple-element.9, f32[1,256,512]{2,1,0:T(8,128)S(1)} %constant_dynamic-slice_fusion.2, bf16[1,1,4,256,512]{4,3,2,1,0:T(8,128)(2,1)} %param.9), kind=kOutput, calls=%fused_computation.22 | convolution fusion | flops 805437440 | bytes 2360320 | tf_op jit(solution)/shard_map/dot_general | solution.py:20
  40.0 5.3 %collective-permute-done.1 = f32[512,512]{1,0:T(8,128)S(1)} collective-permute-done((f32[512,512]{1,0:T(8,128)}, f32[512,512]{1,0:T(8,128)S(1)}, u32[]{:S(2)}, u32[]{:S(2)}) %collective-permute-start.1) | collective-permute-done | bytes 1048608 | tf_op jit(solution)/shard_map/ppermute | solution.py:12
  45.3 1.7 convolution_add_fusion.1
  47.1 1.1 fusion.69
  48.1 2.6 %collective-permute-start.2 = (f32[512,512]{1,0:T(8,128)S(1)}, f32[512,512]{1,0:T(8,128)S(1)}, u32[]{:S(2)}, u32[]{:S(2)}) collective-permute-start(f32[512,512]{1,0:T(8,128)S(1)} %get-tuple-element.10), channel_id=1, source_target_pairs={{0,1},{1,2},{2,3},{3,0},{4,5},{5,6},{6,7},{7,4},{8,9},{9,10},{10,1... | collective-permute-start | bytes 3145736 | tf_op jit(solution)/shard_map/ppermute | solution.py:12
  50.8 1.1 constant_dynamic-slice_fusion.1
  51.9 1.5 fusion.13
  53.4 1.1 constant_dynamic-slice_fusion
  54.5 8.0 %collective-permute-done.2 = f32[512,512]{1,0:T(8,128)S(1)} collective-permute-done((f32[512,512]{1,0:T(8,128)S(1)}, f32[512,512]{1,0:T(8,128)S(1)}, u32[]{:S(2)}, u32[]{:S(2)}) %collective-permute-start.2) | collective-permute-done | bytes 1048608 | tf_op jit(solution)/shard_map/ppermute | solution.py:12
  62.5 1.7 convolution_add_fusion
  64.2 1.1 fusion.70
  65.3 1.5 fusion.11
  66.8 7.3 %scatter_custom_fusion = f32[1536,512]{1,0:T(8,128)} fusion(s32[1024]{0:T(1024)S(1)} %bitcast.141, f32[1024,512]{1,0:T(8,128)} %bitcast.25, f32[]{:T(128)} %constant.98.clone.1), kind=kCustom, calls=%fused_computation.7 | custom fusion | bytes 3146240 | tf_op jit(solution)/shard_map/scatter | solution.py:50
  74.1 5.6 %all-to-all-start = ((f32[8,192,512]{2,1,0:T(8,128)}), f32[8,192,512]{2,1,0:T(8,128)}, u32[]{:S(2)}, u32[]{:S(2)}) async-start(f32[8,192,512]{2,1,0:T(8,128)} %bitcast.135), calls=%async_computation | async-start | bytes 6291456 | tf_op jit(solution)/shard_map/all_to_all | solution.py:52
  79.6 0.0 all-reduce.2.cloned.1.call-start
  79.7 2.8 %collective-permute-start.3 = (f32[512,512]{1,0:T(8,128)S(1)}, f32[512,512]{1,0:T(8,128)}, u32[]{:S(2)}, u32[]{:S(2)}) collective-permute-start(f32[512,512]{1,0:T(8,128)S(1)} %get-tuple-element.12), channel_id=1, source_target_pairs={{0,1},{1,2},{2,3},{3,0},{4,5},{5,6},{6,7},{7,4},{8,9},{9,10},{10,1... | collective-permute-start | bytes 3145736 | tf_op jit(solution)/shard_map/ppermute | solution.py:12
  82.5 66.4 %all-to-all-done = f32[8,192,512]{2,1,0:T(8,128)} async-done(((f32[8,192,512]{2,1,0:T(8,128)}), f32[8,192,512]{2,1,0:T(8,128)}, u32[]{:S(2)}, u32[]{:S(2)}) %all-to-all-start) | async-done | bytes 3145760 | tf_op jit(solution)/shard_map/all_to_all | solution.py:52
  148.8 6.0 %fusion.7 = f32[512,512]{0,1:T(8,128)} fusion(f32[1536,512]{1,0:T(8,128)} %bitcast.27, bf16[1,1,1536,512]{3,2,1,0:T(8,128)(2,1)} %param.12), kind=kOutput, calls=%fused_computation.9 | convolution fusion | flops 4831838208 | bytes 5767168 | tf_op jit(solution)/shard_map/rp,rn->pn/dot_general | solution.py:57
  154.8 0.0 all-reduce.2.cloned.1.call-update
  154.8 0.0 collective-permute-done.3
  154.8 0.0 copy-start.4
  154.9 3.6 %copy.10 = f32[1536,512]{0,1:T(8,128)} copy(f32[1536,512]{1,0:T(8,128)} %bitcast.27) | data formatting | bytes 6291456 | tf_op jit(solution)/shard_map/reshape | solution.py:52
  158.5 32.4 %all-reduce.2.cloned.1.call-done = f32[512,512]{0,1:T(8,128)} async-done(((f32[512,512]{0,1:T(8,128)}), f32[512,512]{0,1:T(8,128)}) %all-reduce.2.cloned.1.call-update) | async-done | bytes 1048592 | tf_op jit(solution)/shard_map/psum | solution.py:58
  190.9 2.3 %fusion.18 = f32[512,512]{1,0:T(8,128)S(1)} fusion(f32[512,512]{0,1:T(8,128)} %all-reduce.2.cloned.1.call-done, bf16[1,512,512]{2,1,0:T(8,128)(2,1)S(1)} %copy-done.4), kind=kOutput, calls=%fused_computation.27 | convolution fusion | flops 1610612736 | bytes 2621440 | tf_op jit(solution)/shard_map/qp,qn->pn/dot_general | solution.py:59
  193.2 0.0 copy-done.3
  193.2 5.6 %fusion.1 = f32[1,1,1536,512]{2,3,1,0:T(8,128)} fusion(f32[1536,512]{0,1:T(8,128)} %copy.10, f32[512,512]{1,0:T(8,128)S(1)} %fusion.18, bf16[1,1,1536,512]{3,2,1,0:T(8,128)(2,1)S(1)} %copy-done.3), kind=kOutput, calls=%fused_computation.3 | convolution fusion | flops 4832624640 | bytes 8912896 | tf_op jit(solution)/shard_map/dot_general | solution.py:60
  198.8 3.5 %copy.11 = f32[1,1,1536,512]{3,2,1,0:T(8,128)} copy(f32[1,1,1536,512]{2,3,1,0:T(8,128)} %fusion.1) | data formatting | bytes 6291456
  202.4 2.3 %copy.20 = f32[1,1,512,512]{3,2,1,0:T(8,128)} copy(f32[1,1,512,512]{3,2,1,0:T(8,128)} %bitcast.17) | data formatting | bytes 2097152
  (8 shorter events, 0.0 us)
Async XLA Ops:
  7.2 2.3 %copy-start = (bf16[1,1,4,512,512]{4,3,2,1,0:T(8,128)(2,1)S(1)}, bf16[1,1,4,512,512]{4,3,2,1,0:T(8,128)(2,1)}, u32[]{:S(2)}) copy-start(bf16[1,1,4,512,512]{4,3,2,1,0:T(8,128)(2,1)} %param.10) | copy-start | bytes 6291460
  7.2 2.4 %copy-start.1 = (f32[1,1,512,512]{3,2,1,0:T(8,128)S(1)}, f32[1,1,512,512]{3,2,1,0:T(8,128)}, u32[]{:S(2)}) copy-start(f32[1,1,512,512]{3,2,1,0:T(8,128)} %param.7) | copy-start | bytes 3145732
  12.0 14.7 %collective-permute-start = (f32[512,512]{1,0:T(8,128)}, f32[512,512]{1,0:T(8,128)S(1)}, u32[]{:S(2)}, u32[]{:S(2)}) collective-permute-start(f32[512,512]{1,0:T(8,128)} %get-tuple-element.6), channel_id=1, source_target_pairs={{0,1},{1,2},{2,3},{3,0},{4,5},{5,6},{6,7},{7,4},{8,9},{9,10},{10,1... | collective-permute-start | bytes 3145736 | tf_op jit(solution)/shard_map/ppermute | solution.py:12
  28.4 4.8 %copy-start.5 = (s32[1,1,1024,1]{2,3,1,0:T(1,128)S(1)}, s32[1,1,1024,1]{2,3,1,0:T(1,128)}, u32[]{:S(2)}) copy-start(s32[1,1,1024,1]{2,3,1,0:T(1,128)} %param.11) | copy-start | bytes 12292
  30.9 14.4 %collective-permute-start.1 = (f32[512,512]{1,0:T(8,128)}, f32[512,512]{1,0:T(8,128)S(1)}, u32[]{:S(2)}, u32[]{:S(2)}) collective-permute-start(f32[512,512]{1,0:T(8,128)} %get-tuple-element.8), channel_id=1, source_target_pairs={{0,1},{1,2},{2,3},{3,0},{4,5},{5,6},{6,7},{7,4},{8,9},{9,10},{10,1... | collective-permute-start | bytes 3145736 | tf_op jit(solution)/shard_map/ppermute | solution.py:12
  36.0 9.3 %copy-start.2 = (bf16[1,1,4,256,512]{4,3,2,1,0:T(8,128)(2,1)S(1)}, bf16[1,1,4,256,512]{4,3,2,1,0:T(8,128)(2,1)}, u32[]{:S(2)}) copy-start(bf16[1,1,4,256,512]{4,3,2,1,0:T(8,128)(2,1)} %param.9) | copy-start | bytes 3145732
  48.1 14.3 %collective-permute-start.2 = (f32[512,512]{1,0:T(8,128)S(1)}, f32[512,512]{1,0:T(8,128)S(1)}, u32[]{:S(2)}, u32[]{:S(2)}) collective-permute-start(f32[512,512]{1,0:T(8,128)S(1)} %get-tuple-element.10), channel_id=1, source_target_pairs={{0,1},{1,2},{2,3},{3,0},{4,5},{5,6},{6,7},{7,4},{8,9},{9,10},{10,1... | collective-permute-start | bytes 3145736 | tf_op jit(solution)/shard_map/ppermute | solution.py:12
  74.1 74.8 %all-to-all-start = ((f32[8,192,512]{2,1,0:T(8,128)}), f32[8,192,512]{2,1,0:T(8,128)}, u32[]{:S(2)}, u32[]{:S(2)}) async-start(f32[8,192,512]{2,1,0:T(8,128)} %bitcast.135), calls=%async_computation | async-start | bytes 6291456 | tf_op jit(solution)/shard_map/all_to_all | solution.py:52
  79.6 111.2 %all-reduce.2.cloned.1.call-start = ((), (), s32[]{:S(2)}) async-start(), calls=%async_computation.1 | async-start | bytes 2097152 | tf_op jit(solution)/shard_map/psum | solution.py:58
  79.7 75.2 %collective-permute-start.3 = (f32[512,512]{1,0:T(8,128)S(1)}, f32[512,512]{1,0:T(8,128)}, u32[]{:S(2)}, u32[]{:S(2)}) collective-permute-start(f32[512,512]{1,0:T(8,128)S(1)} %get-tuple-element.12), channel_id=1, source_target_pairs={{0,1},{1,2},{2,3},{3,0},{4,5},{5,6},{6,7},{7,4},{8,9},{9,10},{10,1... | collective-permute-start | bytes 3145736 | tf_op jit(solution)/shard_map/ppermute | solution.py:12
  154.8 36.0 %copy-start.4 = (bf16[1,512,512]{2,1,0:T(8,128)(2,1)S(1)}, bf16[1,512,512]{2,1,0:T(8,128)(2,1)}, u32[]{:S(2)}) copy-start(bf16[1,512,512]{2,1,0:T(8,128)(2,1)} %param.13) | copy-start | bytes 1572868
  190.9 2.3 %copy-start.3 = (bf16[1,1,1536,512]{3,2,1,0:T(8,128)(2,1)S(1)}, bf16[1,1,1536,512]{3,2,1,0:T(8,128)(2,1)}, u32[]{:S(2)}) copy-start(bf16[1,1,1536,512]{3,2,1,0:T(8,128)(2,1)} %param.12) | copy-start | bytes 4718596
Sparse Core Ops, SparseCore 0:
  155.0 35.8 all-reduce.1
where the time goes:
time: 213 us; the launch traced here: 211 us
  waiting for transfers between devices  118 us (55%)
  matrix products  37.1 us (17%)
  local copies, waits for them, and re-layouts  23.5 us (11%)
  starting transfers between devices  16 us (8%)
  between operations  14.2 us (7%)
  other arithmetic  2.54 us (1%)
    all_to_all x1, waiting for transfers between devices, local(): lax.all_to_all(buffer, 'front', split_axis=0, concat_axis=0, tiled=True)  66.4 us
    psum x1, waiting for transfers between devices, local(): summed = lax.psum(partial_value, 'sect')  32.4 us
    ppermute x4, waiting for transfers between devices, passed_along(): return lax.ppermute(value, axis, pairs)  19.4 us
    ppermute x4, starting transfers between devices, passed_along(): return lax.ppermute(value, axis, pairs)  10.4 us
    unnamed x15, local copies, waits for them, and re-layouts  8.99 us
    dot_general x4, matrix products, reflect(): jnp.dot(vectors, change, precision=highest)  8.65 us
    dot_general x4, matrix products, reflect(): jnp.einsum('rp,rn->pn', vectors, row_block, precision=highest)  7.51 us
    scatter x1, local copies, waits for them, and re-layouts, local(): jnp.zeros((owners * capacity, columns), jnp.float32).at[slot_index]  7.28 us
  transfers between devices with their start and end apart: 6, of which 5 were waited for; matrix products, arithmetic and copies ran while one was open for 12% of the time, Pallas kernels for 0%

commit v1 on v0

v1 whole, which is shorter than its diff:
```python
import jax
import jax.numpy as jnp
from jax import lax
from jax.sharding import PartitionSpec as P

highest = lax.Precision.HIGHEST


def passed_along(value, axis, steps):
    count = lax.axis_size(axis)
    pairs = [(source, (source + steps) % count) for source in range(count)]
    return lax.ppermute(value, axis, pairs)


def reflect(pivot_block, row_block, vectors, factor):
    vectors = vectors.astype(jnp.float32)
    factor = factor.astype(jnp.float32)
    inner_sum = pivot_block + jnp.einsum("rp,rn->pn", vectors, row_block, precision=highest)
    change = jnp.einsum("qp,qn->pn", factor, inner_sum, precision=highest)
    return (pivot_block - change, row_block - jnp.dot(vectors, change, precision=highest))


CHUNKS = 2


def halved_sum(value, axis):
    count = lax.axis_size(axis)
    me = lax.axis_index(axis)
    if count != 4:
        return lax.psum(value, axis)
    near = [(i, i ^ 1) for i in range(count)]
    far = [(i, i ^ 2) for i in range(count)]
    half = value.shape[0] // 2
    odd = me % 2
    mine = lax.dynamic_slice_in_dim(value, odd * half, half, 0)
    other = lax.dynamic_slice_in_dim(value, (1 - odd) * half, half, 0)
    mine = mine + lax.ppermute(other, axis, near)
    mine = mine + lax.ppermute(mine, axis, far)
    other = lax.ppermute(mine, axis, near)
    low = jnp.where(odd == 0, mine, other)
    high = jnp.where(odd == 0, other, mine)
    return jnp.concatenate([low, high], axis=0)


def local(pivot_rows, sections, sect_vectors, sect_factors, routes, parent_vectors, parent_factor):
    owner_index = lax.axis_index("sect")
    owners_sect = lax.axis_size("sect")
    owners = lax.axis_size("front")
    panels, rows, columns = sections.shape[2:]
    row_count = panels * rows
    capacity = 3 * row_count // (2 * owners)
    destination = routes[0, 0, :, 0]
    onehot = (destination[:, None] == jnp.arange(owners, dtype=jnp.int32)[None, :]).astype(
        jnp.int32
    )
    rank_slot = jnp.sum(jnp.cumsum(onehot, axis=0) * onehot, axis=1) - 1
    slot_index = destination * capacity + rank_slot
    order = [(owner_index - step_id) % owners_sect for step_id in range(owners_sect)]
    vectors = [lax.dynamic_index_in_dim(sect_vectors[0, 0], k, 0, keepdims=False) for k in order]
    factors = [lax.dynamic_index_in_dim(sect_factors[0, 0], k, 0, keepdims=False) for k in order]
    slots = slot_index.reshape(panels, rows)
    slots = jnp.concatenate(
        [lax.dynamic_index_in_dim(slots, k, 0, keepdims=False) for k in order], axis=0
    )
    parent_vec = parent_vectors[0, 0].astype(jnp.float32)
    parent_fac = parent_factor[0].astype(jnp.float32)
    width = columns // CHUNKS
    tops, results = [], []
    for chunk in range(CHUNKS):
        cut = slice(chunk * width, (chunk + 1) * width)
        pivot_block = pivot_rows[0, 0, :, cut]
        pieces = []
        for step_id in range(owners_sect):
            row_block = lax.dynamic_index_in_dim(
                sections[0, 0, :, :, cut], order[step_id], 0, keepdims=False
            )
            pivot_block, updated = reflect(
                pivot_block, row_block, vectors[step_id], factors[step_id]
            )
            pieces.append(updated)
            pivot_block = passed_along(pivot_block, "sect", 1)
        contrib = jnp.concatenate(pieces, axis=0)
        buffer = jnp.zeros((owners * capacity, width), jnp.float32).at[slots].set(contrib)
        buffer = buffer.reshape(owners, capacity, width)
        arrived = lax.all_to_all(
            buffer, "front", split_axis=0, concat_axis=0, tiled=True
        ).reshape(owners * capacity, width)
        partial_value = jnp.einsum("rp,rn->pn", parent_vec, arrived, precision=highest)
        summed = halved_sum(partial_value, "sect")
        change = jnp.einsum("qp,qn->pn", parent_fac, summed, precision=highest)
        results.append(arrived - jnp.dot(parent_vec, change, precision=highest))
        tops.append(pivot_block)
    top = jnp.concatenate(tops, axis=1)
    result = jnp.concatenate(results, axis=1)
    return (top[None, None], result[None, None])


def solution(mesh):
    in_specs = (
        P("front", "sect", None, None),
        P("front", "sect", None, None, None),
        P("front", "sect", None, None, None),
        P("front", "sect", None, None, None),
        P("front", "sect", None, None),
        P("front", "sect", None, None),
        P("front", None, None),
    )
    out_specs = (P("front", "sect", None, None), P("front", "sect", None, None))
    return jax.shard_map(local, mesh=mesh, in_specs=in_specs, out_specs=out_specs, check_vma=False)
```

time: 213 us -> 173 us (0.81)
  waiting for transfers between devices: 118 us -> 60.9 us
  other arithmetic: 2.54 us -> 21.5 us
  starting transfers between devices: 16 us -> 31.3 us
  between operations: 14.2 us -> 1.08 us
  local copies, waits for them, and re-layouts: 23.5 us -> 14 us
  matrix products: 37.1 us -> 42.8 us
    psum x1 -> x0, waiting for transfers between devices: 32.4 us -> none  [local(): summed = lax.psum(partial_value, 'sect')]
    all_to_all x1 -> x2, waiting for transfers between devices: 66.4 us -> 34.5 us  [local(): lax.all_to_all(buffer, 'front', split_axis=0, concat_axis=0, tiled=True)]
    scatter x0 -> x2, other arithmetic: none -> 13.5 us  [local(): jnp.zeros((owners * capacity, width), jnp.float32).at[slots].set(contrib)]
    scatter x1 -> x0, local copies, waits for them, and re-layouts: 7.28 us -> none  [local(): jnp.zeros((owners * capacity, columns), jnp.float32).at[slot_index]]
    ppermute x0 -> x6, waiting for transfers between devices: none -> 7.09 us  [the longest x2 6.34 us: halved_sum(): mine = mine + lax.ppermute(mine, axis, far)]
    dot_general x4 -> x8, matrix products: 6.98 us -> 13.1 us  [reflect(): change = jnp.einsum('qp,qn->pn', factor, inner_sum, precision=highest)]
    all_to_all x1 -> x2, starting transfers between devices: 5.56 us -> 11.2 us  [local(): lax.all_to_all(buffer, 'front', split_axis=0, concat_axis=0, tiled=True)]
    ppermute x0 -> x6, starting transfers between devices: none -> 4.85 us  [the longest x2 2.62 us: halved_sum(): mine = mine + lax.ppermute(other, axis, near)]
  transfers between devices with their start and end apart: 6 -> 16, of which waited for: 5 -> 9; matrix products, arithmetic and copies ran while one was open for 12% -> 30% of each run, Pallas kernels for 0% -> 0%
where the time goes in v1:
time: 173 us; the launch traced here: 172 us
  waiting for transfers between devices  60.9 us (35%)
  matrix products  42.8 us (25%)
  starting transfers between devices  31.3 us (18%)
  other arithmetic  21.5 us (12%)
  local copies, waits for them, and re-layouts  14 us (8%)
    all_to_all x2, waiting for transfers between devices, local(): lax.all_to_all(buffer, 'front', split_axis=0, concat_axis=0, tiled=True)  34.5 us
    ppermute x8, waiting for transfers between devices, passed_along(): return lax.ppermute(value, axis, pairs)  19.3 us
    ppermute x8, starting transfers between devices, passed_along(): return lax.ppermute(value, axis, pairs)  15.2 us
    scatter x2, other arithmetic, local(): jnp.zeros((owners * capacity, width), jnp.float32).at[slots].set(contrib)  13.5 us
    dot_general x8, matrix products, reflect(): change = jnp.einsum('qp,qn->pn', factor, inner_sum, precision=highest)  13.1 us
    all_to_all x2, starting transfers between devices, local(): lax.all_to_all(buffer, 'front', split_axis=0, concat_axis=0, tiled=True)  11.2 us
    dot_general x8, matrix products, reflect(): jnp.einsum('rp,rn->pn', vectors, row_block, precision=highest)  9.97 us
    dot_general x8, matrix products, reflect(): jnp.dot(vectors, change, precision=highest)  8.79 us
  transfers between devices with their start and end apart: 16, of which 9 were waited for; matrix products, arithmetic and copies ran while one was open for 30% of the time, Pallas kernels for 0%

profile of v1, /device:TPU:1, one launch (start us, length us, event | category | flops | bytes accessed | tf_op | source)
XLA Modules:
  0.0 171.5 jit_solution(8587283464402385145)
XLA Ops:
  0.7 3.1 %fusion.141 = (f32[1,1,4,256,256]{4,3,2,1,0:T(8,128)}, f32[1,1,4,256,256]{4,3,2,1,0:T(8,128)}) fusion(f32[1,1,4,256,512]{4,3,2,1,0:T(8,128)} %param.8), kind=kLoop, calls=%fused_computation.185 | loop fusion | bytes 4194304 | tf_op jit(solution)/shard_map/slice | solution.py:75
  3.8 1.7 convolution_add_fusion.7
  5.5 1.4 convolution_add_fusion.3
  7.7 1.9 %bitcast_subtract_fusion.1 = (f32[512,256]{1,0:T(8,128)}, f32[512,256]{1,0:T(8,128)}, f32[512,256]{1,0:T(8,128)}) fusion(f32[1,1,512,512]{3,2,1,0:T(8,128)S(1)} %copy-done.9, f32[512,256]{1,0:T(8,128)S(1)} %fusion.48, f32[512,256]{1,0:T(8,128)S(1)} %convolution_add_fusion.7, bf16[1,1,4,512,512]{4,3,2,1,0:T(8,128)(2,1)S(1)} %copy-done, s32[]{:T(128)S(6)} %select_n.97), kind=kOutput, calls=%fused_computation.75 | convolution fusion | flops 805568512 | bytes 4194308 | tf_op jit(solution)/shard_map/qp,qn->pn/dot_general | solution.py:19
  9.6 2.6 %collective-permute-start = (f32[512,256]{1,0:T(8,128)}, f32[512,256]{1,0:T(8,128)}, u32[]{:S(2)}, u32[]{:S(2)}) collective-permute-start(f32[512,256]{1,0:T(8,128)} %get-tuple-element.8), channel_id=1, source_target_pairs={{0,1},{1,2},{2,3},{3,0},{4,5},{5,6},{6,7},{7,4},{8,9},{9,10},{10,1... | collective-permute-start | bytes 1572872 | tf_op jit(solution)/shard_map/ppermute | solution.py:12
  12.3 2.3 %reduce-window.6 = s32[8,8,128]{2,1,0:T(8,128)S(1)} reduce-window(s32[8,8,128]{2,1,0:T(8,128)S(1)} %fusion.110, s32[]{:T(128)} %constant.117.clone.1), window={size=1x1x128 pad=0_0x0_0x127_0}, to_apply=%region_0.0 | reduce-window | flops 1040384 | bytes 65540 | tf_op jit(solution)/shard_map/reduce-window
  15.1 3.6 %collective-permute-done = f32[512,256]{1,0:T(8,128)} collective-permute-done((f32[512,256]{1,0:T(8,128)}, f32[512,256]{1,0:T(8,128)}, u32[]{:S(2)}, u32[]{:S(2)}) %collective-permute-start) | collective-permute-done | bytes 524320 | tf_op jit(solution)/shard_map/ppermute | solution.py:12
  18.7 1.6 convolution_add_fusion.6
  20.2 2.8 %fusion.145 = (f32[512,256]{1,0:T(8,128)}, f32[512,256]{1,0:T(8,128)}) fusion(f32[512,256]{1,0:T(8,128)} %collective-permute-done, f32[512,256]{1,0:T(8,128)S(1)} %convolution_add_fusion.6, bf16[1,1,4,512,512]{4,3,2,1,0:T(8,128)(2,1)S(1)} %copy-done, s32[]{:T(128)S(6)} %select_n.99), kind=kOutput, calls=%fused_computation.189 | convolution fusion | flops 805437440 | bytes 2621444 | tf_op jit(solution)/shard_map/qp,qn->pn/dot_general | solution.py:19
  23.0 2.5 %collective-permute-start.1 = (f32[512,256]{1,0:T(8,128)}, f32[512,256]{1,0:T(8,128)}, u32[]{:S(2)}, u32[]{:S(2)}) collective-permute-start(f32[512,256]{1,0:T(8,128)} %get-tuple-element.25), channel_id=1, source_target_pairs={{0,1},{1,2},{2,3},{3,0},{4,5},{5,6},{6,7},{7,4},{8,9},{9,10},{10,1... | collective-permute-start | bytes 1572872 | tf_op jit(solution)/shard_map/ppermute | solution.py:12
  25.6 1.6 convolution_subtract_fusion.7
  27.2 4.7 %collective-permute-done.1 = f32[512,256]{1,0:T(8,128)} collective-permute-done((f32[512,256]{1,0:T(8,128)}, f32[512,256]{1,0:T(8,128)}, u32[]{:S(2)}, u32[]{:S(2)}) %collective-permute-start.1) | collective-permute-done | bytes 524320 | tf_op jit(solution)/shard_map/ppermute | solution.py:12
  31.9 1.6 convolution_add_fusion.5
  33.5 1.9 %fusion.146 = (f32[512,256]{1,0:T(8,128)S(1)}, f32[512,256]{1,0:T(8,128)S(1)}) fusion(f32[512,256]{1,0:T(8,128)} %collective-permute-done.1, f32[512,256]{1,0:T(8,128)S(1)} %convolution_add_fusion.5, bf16[1,1,4,512,512]{4,3,2,1,0:T(8,128)(2,1)S(1)} %copy-done, s32[]{:T(128)S(6)} %select_n.101), kind=kOutput, calls=%fused_computation.190 | convolution fusion | flops 805437440 | bytes 2621444 | tf_op jit(solution)/shard_map/qp,qn->pn/dot_general | solution.py:19
  35.4 2.5 %collective-permute-start.2 = (f32[512,256]{1,0:T(8,128)S(1)}, f32[512,256]{1,0:T(8,128)S(1)}, u32[]{:S(2)}, u32[]{:S(2)}) collective-permute-start(f32[512,256]{1,0:T(8,128)S(1)} %get-tuple-element.27), channel_id=1, source_target_pairs={{0,1},{1,2},{2,3},{3,0},{4,5},{5,6},{6,7},{7,4},{8,9},{9,10},{10,1... | collective-permute-start | bytes 1572872 | tf_op jit(solution)/shard_map/ppermute | solution.py:12
  39.1 2.4 %convolution_add_fusion.2 = f32[512,256]{1,0:T(8,128)} fusion(f32[512,256]{1,0:T(8,128)} %collective-permute-done.4, f32[1,1,4,256,256]{4,3,2,1,0:T(8,128)} %get-tuple-element.7, s32[]{:T(128)S(6)} %select_n.99, bf16[1,1,4,256,512]{4,3,2,1,0:T(8,128)(2,1)S(1)} %copy-done.2), kind=kOutput, calls=%fused_computation.15 | convolution fusion | flops 402784256 | bytes 1573888 | tf_op jit(solution)/shard_map/rp,rn->pn/dot_general | solution.py:18
  41.5 1.1 convolution_subtract_fusion.5
  42.6 1.5 collective-permute-done.2
  44.5 1.5 fusion.147
  46.1 1.1 convolution_subtract_fusion.4
  47.2 6.7 %scatter_custom_fusion = f32[1536,256]{1,0:T(8,128)} fusion(s32[1024]{0:T(1024)S(1)} %bitcast.199, f32[256,256]{1,0:T(8,128)} %convolution_subtract_fusion.4, f32[]{:T(128)} %constant.141, f32[256,256]{1,0:T(8,128)} %convolution_subtract_fusion.5, f32[256,256]{1,0:T(8,128)} %convolution_subtract_fusion.6, f32[256,256]{1,0:T(8,128)S(1)} %convolution_subtract_fusion.7, ...), kind=kCustom, calls=%fused_computation.30 | custom fusion | flops 786432 | bytes 2621448 | tf_op jit(solution)/shard_map/scatter | solution.py:83
  53.9 5.6 %all-to-all-start = ((f32[8,192,256]{2,1,0:T(8,128)}), f32[8,192,256]{2,1,0:T(8,128)}, u32[]{:S(2)}, u32[]{:S(2)}) async-start(f32[8,192,256]{2,1,0:T(8,128)} %bitcast.195), calls=%async_computation | async-start | bytes 3145728 | tf_op jit(solution)/shard_map/all_to_all | solution.py:85
  59.5 2.0 %fusion.142 = (f32[512,256]{1,0:T(8,128)S(1)}, f32[512,256]{1,0:T(8,128)S(1)}) fusion(f32[512,256]{1,0:T(8,128)} %collective-permute-done.4, f32[512,256]{1,0:T(8,128)} %convolution_add_fusion.2, bf16[1,1,4,512,512]{4,3,2,1,0:T(8,128)(2,1)S(1)} %copy-done, s32[]{:T(128)S(6)} %select_n.99), kind=kOutput, calls=%fused_computation.186 | convolution fusion | flops 805437440 | bytes 2621444 | tf_op jit(solution)/shard_map/qp,qn->pn/dot_general | solution.py:19
  61.5 2.8 %collective-permute-start.5 = (f32[512,256]{1,0:T(8,128)S(1)}, f32[512,256]{1,0:T(8,128)S(1)}, u32[]{:S(2)}, u32[]{:S(2)}) collective-permute-start(f32[512,256]{1,0:T(8,128)S(1)} %get-tuple-element.19), channel_id=1, source_target_pairs={{0,1},{1,2},{2,3},{3,0},{4,5},{5,6},{6,7},{7,4},{8,9},{9,10},{10,1... | collective-permute-start | bytes 1572872 | tf_op jit(solution)/shard_map/ppermute | solution.py:12
  64.4 6.1 %collective-permute-done.5 = f32[512,256]{1,0:T(8,128)S(1)} collective-permute-done((f32[512,256]{1,0:T(8,128)S(1)}, f32[512,256]{1,0:T(8,128)S(1)}, u32[]{:S(2)}, u32[]{:S(2)}) %collective-permute-start.5) | collective-permute-done | bytes 524320 | tf_op jit(solution)/shard_map/ppermute | solution.py:12
  71.7 2.5 %collective-permute-start.6 = (f32[512,256]{1,0:T(8,128)S(1)}, f32[512,256]{1,0:T(8,128)S(1)}, u32[]{:S(2)}, u32[]{:S(2)}) collective-permute-start(f32[512,256]{1,0:T(8,128)S(1)} %get-tuple-element.21), channel_id=1, source_target_pairs={{0,1},{1,2},{2,3},{3,0},{4,5},{5,6},{6,7},{7,4},{8,9},{9,10},{10,1... | collective-permute-start | bytes 1572872 | tf_op jit(solution)/shard_map/ppermute | solution.py:12
  74.7 1.1 convolution_subtract_fusion.2
  75.8 1.1 convolution_subtract_fusion.1
  77.0 3.4 %collective-permute-done.6 = f32[512,256]{1,0:T(8,128)S(1)} collective-permute-done((f32[512,256]{1,0:T(8,128)S(1)}, f32[512,256]{1,0:T(8,128)S(1)}, u32[]{:S(2)}, u32[]{:S(2)}) %collective-permute-start.6) | collective-permute-done | bytes 524320 | tf_op jit(solution)/shard_map/ppermute | solution.py:12
  80.8 1.5 fusion.144
  83.5 6.7 %scatter_custom_fusion.1 = f32[1536,256]{1,0:T(8,128)} fusion(s32[1024]{0:T(1024)S(1)} %bitcast.200, f32[256,256]{1,0:T(8,128)} %convolution_subtract_fusion, f32[]{:T(128)} %constant.141, f32[256,256]{1,0:T(8,128)} %convolution_subtract_fusion.1, f32[256,256]{1,0:T(8,128)} %convolution_subtract_fusion.2, f32[256,256]{1,0:T(8,128)S(1)} %convolution_subtract_fusion.3, ...), kind=kCustom, calls=%fused_computation.38 | custom fusion | flops 786432 | bytes 2621448 | tf_op jit(solution)/shard_map/scatter | solution.py:83
  90.2 4.5 %all-to-all-done = f32[8,192,256]{2,1,0:T(8,128)} async-done(((f32[8,192,256]{2,1,0:T(8,128)}), f32[8,192,256]{2,1,0:T(8,128)}, u32[]{:S(2)}, u32[]{:S(2)}) %all-to-all-start) | async-done | bytes 1572896 | tf_op jit(solution)/shard_map/all_to_all | solution.py:85
  94.7 5.6 %all-to-all-start.1 = ((f32[8,192,256]{2,1,0:T(8,128)}), f32[8,192,256]{2,1,0:T(8,128)}, u32[]{:S(2)}, u32[]{:S(2)}) async-start(f32[8,192,256]{2,1,0:T(8,128)} %bitcast.194), calls=%async_computation.1 | async-start | bytes 3145728 | tf_op jit(solution)/shard_map/all_to_all | solution.py:85
  100.4 1.9 %collective-permute-start.3 = (f32[512,256]{1,0:T(8,128)}, f32[512,256]{1,0:T(8,128)}, u32[]{:S(2)}, u32[]{:S(2)}) collective-permute-start(f32[512,256]{1,0:T(8,128)} %get-tuple-element.29), channel_id=1, source_target_pairs={{0,1},{1,2},{2,3},{3,0},{4,5},{5,6},{6,7},{7,4},{8,9},{9,10},{10,1... | collective-permute-start | bytes 1572872 | tf_op jit(solution)/shard_map/ppermute | solution.py:12
  102.6 3.3 %fusion.6 = f32[256,512]{1,0:T(8,128)S(1)} fusion(f32[1536,256]{1,0:T(8,128)} %bitcast.28, bf16[1,1,1536,512]{3,2,1,0:T(8,128)(2,1)} %param.12), kind=kOutput, calls=%fused_computation.11 | convolution fusion | flops 2415919104 | bytes 3670016 | tf_op jit(solution)/shard_map/rp,rn->pn/dot_general | solution.py:88
  106.2 30.0 %all-to-all-done.1 = f32[8,192,256]{2,1,0:T(8,128)} async-done(((f32[8,192,256]{2,1,0:T(8,128)}), f32[8,192,256]{2,1,0:T(8,128)}, u32[]{:S(2)}, u32[]{:S(2)}) %all-to-all-start.1) | async-done | bytes 1572896 | tf_op jit(solution)/shard_map/all_to_all | solution.py:85
  136.2 3.3 %fusion.3 = f32[256,512]{1,0:T(8,128)S(1)} fusion(f32[1536,256]{1,0:T(8,128)} %bitcast.35, bf16[1,1,1536,512]{3,2,1,0:T(8,128)(2,1)} %param.12), kind=kOutput, calls=%fused_computation.8 | convolution fusion | flops 2415919104 | bytes 3670016 | tf_op jit(solution)/shard_map/rp,rn->pn/dot_general | solution.py:88
  139.6 2.3 %collective-permute-start.11 = (f32[256,256]{0,1:T(8,128)S(1)}, f32[256,256]{0,1:T(8,128)S(1)}, u32[]{:S(2)}, u32[]{:S(2)}) collective-permute-start(f32[256,256]{0,1:T(8,128)S(1)} %dynamic-slice_bitcast_fusion), channel_id=1, source_target_pairs={{0,1},{1,0},{2,3},{3,2},{4,5},{5,4},{6,7},{7,6},{8,9},{9,8},{10,11... | collective-permute-start | bytes 786440 | tf_op jit(solution)/shard_map/ppermute | solution.py:37
  143.6 6.3 %collective-permute-done.9 = f32[256,256]{0,1:T(8,128)S(1)} collective-permute-done((f32[256,256]{0,1:T(8,128)S(1)}, f32[256,256]{0,1:T(8,128)S(1)}, u32[]{:S(2)}, u32[]{:S(2)}) %collective-permute-start.9) | collective-permute-done | bytes 262176 | tf_op jit(solution)/shard_map/ppermute | solution.py:38
  150.0 1.3 collective-permute-start.10
  151.2 2.3 %maximum_bitcast_fusion.1 = f32[1,1,512,512]{3,2,1,0:T(8,128)} fusion(f32[512,256]{1,0:T(8,128)} %collective-permute-done.7, f32[512,256]{1,0:T(8,128)} %collective-permute-done.3), kind=kLoop, calls=%fused_computation.29 | loop fusion | flops 262144 | bytes 2097152 | tf_op jit(solution)/shard_map/broadcast_in_dim | solution.py:95
  153.5 3.0 %copy.10 = f32[1536,256]{0,1:T(8,128)} copy(f32[1536,256]{1,0:T(8,128)} %bitcast.28) | data formatting | bytes 3145728 | tf_op jit(solution)/shard_map/reshape | solution.py:87
  156.6 3.1 %copy.11 = f32[1536,256]{0,1:T(8,128)} copy(f32[1536,256]{1,0:T(8,128)} %bitcast.35) | data formatting | bytes 3145728 | tf_op jit(solution)/shard_map/reshape | solution.py:87
  159.8 1.1 broadcast_select_fusion.3
  161.6 1.6 fusion.1
  164.6 1.6 fusion
  166.2 1.8 %maximum_bitcast_fusion = f32[1,1,1536,512]{2,3,1,0:T(8,128)} fusion(f32[1536,256]{0,1:T(8,128)S(1)} %fusion, f32[1536,256]{0,1:T(8,128)S(1)} %fusion.1), kind=kLoop, calls=%fused_computation.2 | loop fusion | flops 786432 | bytes 6291456 | tf_op jit(solution)/shard_map/broadcast_in_dim | solution.py:95
  168.0 3.5 %copy.12 = f32[1,1,1536,512]{3,2,1,0:T(8,128)} copy(f32[1,1,1536,512]{2,3,1,0:T(8,128)} %maximum_bitcast_fusion) | data formatting | bytes 6291456
  (69 shorter events, 10.8 us)
Async XLA Ops:
  0.6 6.3 %copy-start = (bf16[1,1,4,512,512]{4,3,2,1,0:T(8,128)(2,1)S(1)}, bf16[1,1,4,512,512]{4,3,2,1,0:T(8,128)(2,1)}, u32[]{:S(2)}) copy-start(bf16[1,1,4,512,512]{4,3,2,1,0:T(8,128)(2,1)} %param.10) | copy-start | bytes 6291460
  0.7 3.2 %copy-start.2 = (bf16[1,1,4,256,512]{4,3,2,1,0:T(8,128)(2,1)S(1)}, bf16[1,1,4,256,512]{4,3,2,1,0:T(8,128)(2,1)}, u32[]{:S(2)}) copy-start(bf16[1,1,4,256,512]{4,3,2,1,0:T(8,128)(2,1)} %param.9) | copy-start | bytes 3145732
  3.8 1.7 copy-start.9
  7.7 1.9 %copy-start.7 = (f32[512,256]{1,0:T(8,128)}, f32[512,256]{1,0:T(8,128)S(1)}, u32[]{:S(2)}) copy-start(f32[512,256]{1,0:T(8,128)S(1)} %fusion.48) | copy-start | bytes 1572868
  7.7 4.6 %copy-start.12 = (s32[1,1,1024,1]{2,3,1,0:T(1,128)S(1)}, s32[1,1,1024,1]{2,3,1,0:T(1,128)}, u32[]{:S(2)}) copy-start(s32[1,1,1024,1]{2,3,1,0:T(1,128)} %param.11) | copy-start | bytes 12292
  9.6 9.0 %collective-permute-start = (f32[512,256]{1,0:T(8,128)}, f32[512,256]{1,0:T(8,128)}, u32[]{:S(2)}, u32[]{:S(2)}) collective-permute-start(f32[512,256]{1,0:T(8,128)} %get-tuple-element.8), channel_id=1, source_target_pairs={{0,1},{1,2},{2,3},{3,0},{4,5},{5,6},{6,7},{7,4},{8,9},{9,10},{10,1... | collective-permute-start | bytes 1572872 | tf_op jit(solution)/shard_map/ppermute | solution.py:12
  12.2 26.9 %collective-permute-start.4 = (f32[512,256]{1,0:T(8,128)}, f32[512,256]{1,0:T(8,128)}, u32[]{:S(2)}, u32[]{:S(2)}) collective-permute-start(f32[512,256]{1,0:T(8,128)} %get-tuple-element.9), channel_id=1, source_target_pairs={{0,1},{1,2},{2,3},{3,0},{4,5},{5,6},{6,7},{7,4},{8,9},{9,10},{10,1... | collective-permute-start | bytes 1572872 | tf_op jit(solution)/shard_map/ppermute | solution.py:12
  23.0 8.9 %collective-permute-start.1 = (f32[512,256]{1,0:T(8,128)}, f32[512,256]{1,0:T(8,128)}, u32[]{:S(2)}, u32[]{:S(2)}) collective-permute-start(f32[512,256]{1,0:T(8,128)} %get-tuple-element.25), channel_id=1, source_target_pairs={{0,1},{1,2},{2,3},{3,0},{4,5},{5,6},{6,7},{7,4},{8,9},{9,10},{10,1... | collective-permute-start | bytes 1572872 | tf_op jit(solution)/shard_map/ppermute | solution.py:12
  33.5 4.5 %copy-start.4 = (f32[1,1,4,256,256]{4,3,2,1,0:T(8,128)S(1)}, f32[1,1,4,256,256]{4,3,2,1,0:T(8,128)}, u32[]{:S(2)}) copy-start(f32[1,1,4,256,256]{4,3,2,1,0:T(8,128)} %get-tuple-element.6) | copy-start | bytes 3145732
  33.5 4.4 %copy-start.11 = (f32[512,256]{1,0:T(8,128)S(1)}, f32[512,256]{1,0:T(8,128)}, u32[]{:S(2)}) copy-start(f32[512,256]{1,0:T(8,128)} %get-tuple-element.26) | copy-start | bytes 1572868
  35.4 8.7 %collective-permute-start.2 = (f32[512,256]{1,0:T(8,128)S(1)}, f32[512,256]{1,0:T(8,128)S(1)}, u32[]{:S(2)}, u32[]{:S(2)}) collective-permute-start(f32[512,256]{1,0:T(8,128)S(1)} %get-tuple-element.27), channel_id=1, source_target_pairs={{0,1},{1,2},{2,3},{3,0},{4,5},{5,6},{6,7},{7,4},{8,9},{9,10},{10,1... | collective-permute-start | bytes 1572872 | tf_op jit(solution)/shard_map/ppermute | solution.py:12
  53.9 40.8 %all-to-all-start = ((f32[8,192,256]{2,1,0:T(8,128)}), f32[8,192,256]{2,1,0:T(8,128)}, u32[]{:S(2)}, u32[]{:S(2)}) async-start(f32[8,192,256]{2,1,0:T(8,128)} %bitcast.195), calls=%async_computation | async-start | bytes 3145728 | tf_op jit(solution)/shard_map/all_to_all | solution.py:85
  59.5 11.0 %copy-start.3 = (f32[1,1,4,256,256]{4,3,2,1,0:T(8,128)S(1)}, f32[1,1,4,256,256]{4,3,2,1,0:T(8,128)}, u32[]{:S(2)}) copy-start(f32[1,1,4,256,256]{4,3,2,1,0:T(8,128)} %get-tuple-element.7) | copy-start | bytes 3145732
  61.5 8.9 %collective-permute-start.5 = (f32[512,256]{1,0:T(8,128)S(1)}, f32[512,256]{1,0:T(8,128)S(1)}, u32[]{:S(2)}, u32[]{:S(2)}) collective-permute-start(f32[512,256]{1,0:T(8,128)S(1)} %get-tuple-element.19), channel_id=1, source_target_pairs={{0,1},{1,2},{2,3},{3,0},{4,5},{5,6},{6,7},{7,4},{8,9},{9,10},{10,1... | collective-permute-start | bytes 1572872 | tf_op jit(solution)/shard_map/ppermute | solution.py:12
  71.0 3.3 %copy-start.8 = (f32[512,256]{1,0:T(8,128)S(1)}, f32[512,256]{1,0:T(8,128)}, u32[]{:S(2)}) copy-start(f32[512,256]{1,0:T(8,128)} %copy-done.7) | copy-start | bytes 1572868
  71.7 8.7 %collective-permute-start.6 = (f32[512,256]{1,0:T(8,128)S(1)}, f32[512,256]{1,0:T(8,128)S(1)}, u32[]{:S(2)}, u32[]{:S(2)}) collective-permute-start(f32[512,256]{1,0:T(8,128)S(1)} %get-tuple-element.21), channel_id=1, source_target_pairs={{0,1},{1,2},{2,3},{3,0},{4,5},{5,6},{6,7},{7,4},{8,9},{9,10},{10,1... | collective-permute-start | bytes 1572872 | tf_op jit(solution)/shard_map/ppermute | solution.py:12
  94.7 41.5 %all-to-all-start.1 = ((f32[8,192,256]{2,1,0:T(8,128)}), f32[8,192,256]{2,1,0:T(8,128)}, u32[]{:S(2)}, u32[]{:S(2)}) async-start(f32[8,192,256]{2,1,0:T(8,128)} %bitcast.194), calls=%async_computation.1 | async-start | bytes 3145728 | tf_op jit(solution)/shard_map/all_to_all | solution.py:85
  100.4 50.8 %collective-permute-start.3 = (f32[512,256]{1,0:T(8,128)}, f32[512,256]{1,0:T(8,128)}, u32[]{:S(2)}, u32[]{:S(2)}) collective-permute-start(f32[512,256]{1,0:T(8,128)} %get-tuple-element.29), channel_id=1, source_target_pairs={{0,1},{1,2},{2,3},{3,0},{4,5},{5,6},{6,7},{7,4},{8,9},{9,10},{10,1... | collective-permute-start | bytes 1572872 | tf_op jit(solution)/shard_map/ppermute | solution.py:12
  102.3 48.9 %collective-permute-start.7 = (f32[512,256]{1,0:T(8,128)}, f32[512,256]{1,0:T(8,128)}, u32[]{:S(2)}, u32[]{:S(2)}) collective-permute-start(f32[512,256]{1,0:T(8,128)} %get-tuple-element.23), channel_id=1, source_target_pairs={{0,1},{1,2},{2,3},{3,0},{4,5},{5,6},{6,7},{7,4},{8,9},{9,10},{10,1... | collective-permute-start | bytes 1572872 | tf_op jit(solution)/shard_map/ppermute | solution.py:12
  106.0 35.9 %collective-permute-start.8 = (f32[256,256]{0,1:T(8,128)S(1)}, f32[256,256]{0,1:T(8,128)S(1)}, u32[]{:S(2)}, u32[]{:S(2)}) collective-permute-start(f32[256,256]{0,1:T(8,128)S(1)} %dynamic-slice_bitcast_fusion.1), channel_id=1, source_target_pairs={{0,1},{1,0},{2,3},{3,2},{4,5},{5,4},{6,7},{7,6},{8,9},{9,8},{10,11... | collective-permute-start | bytes 786440 | tf_op jit(solution)/shard_map/ppermute | solution.py:37
  139.6 3.5 %collective-permute-start.11 = (f32[256,256]{0,1:T(8,128)S(1)}, f32[256,256]{0,1:T(8,128)S(1)}, u32[]{:S(2)}, u32[]{:S(2)}) collective-permute-start(f32[256,256]{0,1:T(8,128)S(1)} %dynamic-slice_bitcast_fusion), channel_id=1, source_target_pairs={{0,1},{1,0},{2,3},{3,2},{4,5},{5,4},{6,7},{7,6},{8,9},{9,8},{10,11... | collective-permute-start | bytes 786440 | tf_op jit(solution)/shard_map/ppermute | solution.py:37
  141.9 8.0 %collective-permute-start.9 = (f32[256,256]{0,1:T(8,128)S(1)}, f32[256,256]{0,1:T(8,128)S(1)}, u32[]{:S(2)}, u32[]{:S(2)}) collective-permute-start(f32[256,256]{0,1:T(8,128)S(1)} %bitcast_add_fusion.1), channel_id=1, source_target_pairs={{0,2},{1,3},{2,0},{3,1},{4,6},{5,7},{6,4},{7,5},{8,10},{9,11},{10,... | collective-permute-start | bytes 786440 | tf_op jit(solution)/shard_map/ppermute | solution.py:38
  143.1 16.6 %collective-permute-start.12 = (f32[256,256]{0,1:T(8,128)S(1)}, f32[256,256]{0,1:T(8,128)S(1)}, u32[]{:S(2)}, u32[]{:S(2)}) collective-permute-start(f32[256,256]{0,1:T(8,128)S(1)} %bitcast_add_fusion), channel_id=1, source_target_pairs={{0,2},{1,3},{2,0},{3,1},{4,6},{5,7},{6,4},{7,5},{8,10},{9,11},{10,... | collective-permute-start | bytes 786440 | tf_op jit(solution)/shard_map/ppermute | solution.py:38
  150.0 9.8 %collective-permute-start.10 = (f32[256,256]{0,1:T(8,128)S(1)}, f32[256,256]{0,1:T(8,128)}, u32[]{:S(2)}, u32[]{:S(2)}) collective-permute-start(f32[256,256]{0,1:T(8,128)S(1)} %add.136), channel_id=1, source_target_pairs={{0,1},{1,0},{2,3},{3,2},{4,5},{5,4},{6,7},{7,6},{8,9},{9,8},{10,11... | collective-permute-start | bytes 786440 | tf_op jit(solution)/shard_map/ppermute | solution.py:39
  156.6 4.4 %copy-start.10 = (bf16[1,512,512]{2,1,0:T(8,128)(2,1)S(1)}, bf16[1,512,512]{2,1,0:T(8,128)(2,1)}, u32[]{:S(2)}) copy-start(bf16[1,512,512]{2,1,0:T(8,128)(2,1)} %param.13) | copy-start | bytes 1572868
  159.6 1.9 %copy-start.1 = (bf16[1,1,1536,512]{3,2,1,0:T(8,128)(2,1)S(1)}, bf16[1,1,1536,512]{3,2,1,0:T(8,128)(2,1)}, u32[]{:S(2)}) copy-start(bf16[1,1,1536,512]{3,2,1,0:T(8,128)(2,1)} %param.12) | copy-start | bytes 4718596
  159.6 2.0 %copy-start.6 = (f32[1536,256]{0,1:T(8,128)S(1)}, f32[1536,256]{0,1:T(8,128)}, u32[]{:S(2)}) copy-start(f32[1536,256]{0,1:T(8,128)} %copy.10) | copy-start | bytes 4718596
  159.7 3.5 %collective-permute-start.13 = (f32[256,256]{0,1:T(8,128)S(1)}, f32[256,256]{0,1:T(8,128)S(1)}, u32[]{:S(2)}, u32[]{:S(2)}) collective-permute-start(f32[256,256]{0,1:T(8,128)S(1)} %add.138), channel_id=1, source_target_pairs={{0,1},{1,0},{2,3},{3,2},{4,5},{5,4},{6,7},{7,6},{8,9},{9,8},{10,11... | collective-permute-start | bytes 786440 | tf_op jit(solution)/shard_map/ppermute | solution.py:39
  163.2 1.4 copy-start.5

commit v2 on v0

v2 whole, which is shorter than its diff:
```python
import functools

import jax
import jax.numpy as jnp
from jax import lax
from jax.experimental import pallas as pl
from jax.experimental.pallas import tpu as pltpu
from jax.sharding import PartitionSpec as P

MESH = pl.DeviceIdType.MESH
WIDTH = 128
TILE = 256
F32 = jnp.float32
BF16 = jnp.bfloat16


def halves(value):
    high = value.astype(BF16)
    low = (value - high.astype(F32)).astype(BF16)
    return jnp.concatenate([high, low], axis=1)


def joined(value):
    return value[:, :WIDTH] + value[:, WIDTH:]


def dot(left, right):
    return joined(jnp.dot(left, right, preferred_element_type=F32))


def dot_t(left, right):
    return joined(
        lax.dot_general(left, right, (((0,), (0,)), ((), ())), preferred_element_type=F32)
    )


def kernel(
    owners, steps, chunks,
    pivot_ref, sect_ref, y_ref, t_ref, route_ref, v_ref, f_ref,
    top_ref, out_ref,
    place, slot_row, pivots, pivots_out, contrib, send, arrived, arrived_cat,
    vt, ft, part, part_near, pair, pair_far, total,
    chain_send, chain_recv, swap_send, swap_recv, sum_send, sum_recv,
):
    front = lax.axis_index("front")
    me = lax.axis_index("sect")
    rows = sect_ref.shape[1]
    row_count = sect_ref.shape[0] * rows
    slots = v_ref.shape[0]
    capacity = slots // owners
    depth = pivot_ref.shape[0]
    half = depth // 2
    lag = steps // 2
    odd = lax.rem(me, 2)
    near = me + 1 - 2 * odd
    far = me + 2 - 4 * lax.rem(me // 2, 2)
    right = lax.rem(me + 1, steps)

    def peer(m):
        found = 0
        bit = 1
        while bit < owners:
            found = found + bit * lax.rem(front // bit + m // bit, 2)
            bit *= 2
        return found

    barrier = pltpu.get_barrier_semaphore()

    @pl.loop(1, owners)
    def _(m):
        pl.semaphore_signal(barrier, inc=1, device_id={"front": peer(m)}, device_id_type=MESH)

    for shift in range(1, steps):
        pl.semaphore_signal(
            barrier, inc=1, device_id={"sect": lax.rem(me + shift, steps)}, device_id_type=MESH
        )

    lanes = 128
    before = (
        lax.broadcasted_iota(jnp.int32, (lanes, lanes), 0)
        <= lax.broadcasted_iota(jnp.int32, (lanes, lanes), 1)
    ).astype(F32)
    owner_ids = lax.broadcasted_iota(jnp.int32, (owners, lanes), 0)
    carry = jnp.zeros((owners, 1), F32)
    for group in range(row_count // lanes):
        cut = slice(group * lanes, (group + 1) * lanes)
        named = route_ref[:, cut]
        hit = (owner_ids == named).astype(F32)
        count = jnp.dot(hit, before, preferred_element_type=F32) + carry
        rank = jnp.sum(hit * count, axis=0, keepdims=True) - 1.0
        slot_row[:, cut] = named.astype(F32) * float(capacity) + rank
        carry = carry + jnp.sum(hit, axis=1, keepdims=True)

    @pl.loop(0, slots // TILE)
    def _(tile):
        ids = lax.broadcasted_iota(jnp.int32, (TILE, row_count), 0) + tile * TILE
        hit = ids.astype(F32) == slot_row[...]
        place[pl.ds(pl.multiple_of(tile * TILE, TILE), TILE), :] = hit.astype(F32).astype(BF16)

    pl.semaphore_wait(barrier, owners - 1 + steps - 1)

    def columns(chunk):
        return pl.ds(pl.multiple_of(chunk * WIDTH, WIDTH), WIDTH)

    def chain_copy(chunk, step):
        return pltpu.make_async_remote_copy(
            src_ref=pivots_out.at[chunk * steps + step],
            dst_ref=pivots.at[chunk * steps + step],
            send_sem=chain_send.at[chunk * steps + step],
            recv_sem=chain_recv.at[chunk * steps + step],
            device_id={"sect": right},
            device_id_type=MESH,
        )

    def swap_copy(chunk, m):
        to = peer(m)
        return pltpu.make_async_remote_copy(
            src_ref=send.at[chunk, pl.ds(pl.multiple_of(to * capacity, 8), capacity)],
            dst_ref=arrived.at[chunk, pl.ds(pl.multiple_of(front * capacity, 8), capacity)],
            send_sem=swap_send.at[chunk],
            recv_sem=swap_recv.at[chunk],
            device_id={"front": to},
            device_id_type=MESH,
        )

    def reflect(chunk, step, pivot_block):
        panel = lax.rem(me - step + steps, steps)
        row_block = sect_ref[panel, :, columns(chunk)]
        vectors = y_ref[panel]
        inner = pivot_block + dot_t(vectors, halves(row_block))
        change = dot_t(t_ref[panel], halves(inner))
        pivots_out[chunk * steps + step] = pivot_block - change
        chain_copy(chunk, step).start()
        updated = row_block - dot(vectors, halves(change))
        contrib[chunk, pl.ds(pl.multiple_of(panel * rows, rows), rows), :] = halves(updated)

    def later_step(chunk, step):
        chain_copy(chunk, step - 1).wait_recv()
        reflect(chunk, step, pivots[chunk * steps + step - 1])

    def exchange(chunk):
        @pl.loop(0, slots // TILE)
        def _(tile):
            cut = pl.ds(pl.multiple_of(tile * TILE, TILE), TILE)
            send[chunk, cut, :] = dot(place[cut, :], contrib[chunk])

        @pl.loop(1, owners)
        def _(m):
            swap_copy(chunk, owners - m).start()

        own = pl.ds(pl.multiple_of(front * capacity, 8), capacity)
        arrived[chunk, own, :] = send[chunk, own, :]

    @pl.loop(0, lag * (chunks + 1))
    def _(slot):
        within = lax.rem(slot, lag)

        @pl.when(slot >= lag)
        def _():
            later_step(slot // lag - 1, within + lag)

            @pl.when(within == lag - 1)
            def _():
                exchange(slot // lag - 1)

        @pl.when(slot < lag * chunks)
        def _():
            @pl.when(within == 0)
            def _():
                reflect(slot // lag, 0, pivot_ref[:, columns(slot // lag)])

            @pl.when(within > 0)
            def _():
                later_step(slot // lag, within)

    @pl.loop(0, slots // TILE)
    def _(tile):
        cut = pl.ds(pl.multiple_of(tile * TILE, TILE), TILE)
        vt[:, cut] = v_ref[cut, :].T

    ft[...] = f_ref[...].T

    @pl.loop(0, chunks)
    def _(chunk):
        chain_copy(chunk, steps - 1).wait_recv()
        top_ref[:, columns(chunk)] = pivots[chunk * steps + steps - 1]

    def sum_copy(chunk, stage, source, target, to):
        return pltpu.make_async_remote_copy(
            src_ref=source,
            dst_ref=target,
            send_sem=sum_send.at[chunk * 3 + stage],
            recv_sem=sum_recv.at[chunk * 3 + stage],
            device_id={"sect": to},
            device_id_type=MESH,
        )

    mine = pl.ds(pl.multiple_of(odd * half, half), half)
    other = pl.ds(pl.multiple_of((1 - odd) * half, half), half)

    def sum_copies(chunk):
        return (
            sum_copy(chunk, 0, part.at[chunk, other], part_near.at[chunk], near),
            sum_copy(chunk, 1, pair.at[chunk], pair_far.at[chunk], far),
            sum_copy(chunk, 2, total.at[chunk, mine], total.at[chunk, mine], near),
        )

    def swapped(chunk, sem):
        whole = send.at[chunk, pl.ds(0, (owners - 1) * capacity)]
        return pltpu.make_async_copy(whole, whole, sem.at[chunk])

    @pl.loop(0, chunks)
    def _(chunk):
        swapped(chunk, swap_recv).wait()
        first, second, third = sum_copies(chunk)

        @pl.loop(0, slots // TILE)
        def _(tile):
            cut = pl.ds(pl.multiple_of(tile * TILE, TILE), TILE)
            arrived_cat[cut, :] = halves(arrived[chunk, cut, :])

        part[chunk, other, :] = dot(vt[other, :], arrived_cat[...])
        first.start()
        part[chunk, mine, :] = dot(vt[mine, :], arrived_cat[...])
        first.wait_recv()
        pair[chunk] = part[chunk, mine, :] + part_near[chunk]
        second.start()
        second.wait_recv()
        total[chunk, mine, :] = pair[chunk] + pair_far[chunk]
        third.start()
        third.wait_recv()
        change = halves(dot(ft[...], halves(total[chunk])))

        @pl.loop(0, slots // TILE)
        def _(tile):
            cut = pl.ds(pl.multiple_of(tile * TILE, TILE), TILE)
            out_ref[cut, columns(chunk)] = arrived[chunk, cut, :] - dot(v_ref[cut, :], change)

    @pl.loop(0, chunks)
    def _(chunk):
        for copy in sum_copies(chunk):
            copy.wait_send()
        swapped(chunk, swap_send).wait()

    @pl.loop(0, chunks * steps)
    def _(index):
        chain_copy(index // steps, lax.rem(index, steps)).wait_send()


def local(pivot_rows, sections, sect_vectors, sect_factors, routes, parent_vectors, parent_factor):
    owners = lax.axis_size("front")
    steps = lax.axis_size("sect")
    panels, rows, columns = sections.shape[2:]
    depth = pivot_rows.shape[2]
    slots = parent_vectors.shape[2]
    row_count = panels * rows
    chunks = columns // WIDTH
    half = depth // 2
    vmem = pl.BlockSpec(memory_space=pltpu.VMEM)
    dma = pltpu.SemaphoreType.DMA
    top, result = pl.pallas_call(
        functools.partial(kernel, owners, steps, chunks),
        out_shape=(
            jax.ShapeDtypeStruct((depth, columns), F32),
            jax.ShapeDtypeStruct((slots, columns), F32),
        ),
        in_specs=[vmem] * 7,
        out_specs=(vmem, vmem),
        scratch_shapes=[
            pltpu.VMEM((slots, row_count), BF16),
            pltpu.VMEM((1, row_count), F32),
            pltpu.VMEM((chunks * steps, depth, WIDTH), F32),
            pltpu.VMEM((chunks * steps, depth, WIDTH), F32),
            pltpu.VMEM((chunks, row_count, 2 * WIDTH), BF16),
            pltpu.VMEM((chunks, slots, WIDTH), F32),
            pltpu.VMEM((chunks, slots, WIDTH), F32),
            pltpu.VMEM((slots, 2 * WIDTH), BF16),
            pltpu.VMEM((depth, slots), BF16),
            pltpu.VMEM((depth, depth), BF16),
            pltpu.VMEM((chunks, depth, WIDTH), F32),
            pltpu.VMEM((chunks, half, WIDTH), F32),
            pltpu.VMEM((chunks, half, WIDTH), F32),
            pltpu.VMEM((chunks, half, WIDTH), F32),
            pltpu.VMEM((chunks, depth, WIDTH), F32),
            dma((chunks * steps,)),
            dma((chunks * steps,)),
            dma((chunks,)),
            dma((chunks,)),
            dma((chunks * 3,)),
            dma((chunks * 3,)),
        ],
        compiler_params=pltpu.CompilerParams(
            collective_id=0, has_side_effects=True, vmem_limit_bytes=50 * 2**20
        ),
        cost_estimate=pl.CostEstimate(
            flops=8 * 10**9, bytes_accessed=12 * 2**20, transcendentals=0
        ),
    )(
        pivot_rows[0, 0],
        sections[0, 0],
        sect_vectors[0, 0],
        sect_factors[0, 0],
        routes[0, 0].reshape(1, row_count),
        parent_vectors[0, 0],
        parent_factor[0],
    )
    return (top[None, None], result[None, None])


def solution(mesh):
    in_specs = (
        P("front", "sect", None, None),
        P("front", "sect", None, None, None),
        P("front", "sect", None, None, None),
        P("front", "sect", None, None, None),
        P("front", "sect", None, None),
        P("front", "sect", None, None),
        P("front", None, None),
    )
    out_specs = (P("front", "sect", None, None), P("front", "sect", None, None))
    return jax.shard_map(local, mesh=mesh, in_specs=in_specs, out_specs=out_specs, check_vma=False)
```

time: 213 us -> 114 us (0.54)
  waiting for transfers between devices: 118 us -> 0 us
  Pallas kernels: 0 us -> 104 us
  matrix products: 37.1 us -> 0 us
  starting transfers between devices: 16 us -> 0 us
  local copies, waits for them, and re-layouts: 23.5 us -> 9 us
  between operations: 14.2 us -> 0.65 us
  other arithmetic: 2.54 us -> 0 us
    pallas_call x0 -> x1, Pallas kernels: none -> 104 us  [local(): pl.pallas_call(functools.partial(kernel, owners, steps, chunks), out_shap...]
    all_to_all x1 -> x0, waiting for transfers between devices: 66.4 us -> none  [local(): lax.all_to_all(buffer, 'front', split_axis=0, concat_axis=0, tiled=True)]
    dot_general x15 -> x0, matrix products: 37.1 us -> none  [the longest x4 8.65 us: reflect(): jnp.dot(vectors, change, precision=highest)]
    psum x1 -> x0, waiting for transfers between devices: 32.4 us -> none  [local(): summed = lax.psum(partial_value, 'sect')]
    ppermute x4 -> x0, waiting for transfers between devices: 19.4 us -> none  [passed_along(): return lax.ppermute(value, axis, pairs)]
    ppermute x4 -> x0, starting transfers between devices: 10.4 us -> none  [passed_along(): return lax.ppermute(value, axis, pairs)]
    scatter x1 -> x0, local copies, waits for them, and re-layouts: 7.28 us -> none  [local(): jnp.zeros((owners * capacity, columns), jnp.float32).at[slot_index]]
    all_to_all x1 -> x0, starting transfers between devices: 5.56 us -> none  [local(): lax.all_to_all(buffer, 'front', split_axis=0, concat_axis=0, tiled=True)]
  transfers between devices with their start and end apart: 6 -> 0, of which waited for: 5 -> 0; matrix products, arithmetic and copies ran while one was open for 12% -> 0% of each run, Pallas kernels for 0% -> 0%
where the time goes in v2:
time: 114 us
  Pallas kernels  104 us (91%)
  local copies, waits for them, and re-layouts  9 us (8%)
    pallas_call x1, Pallas kernels, local(): pl.pallas_call(functools.partial(kernel, owners, steps, chunks), out_shap...  104 us
    unnamed x10, local copies, waits for them, and re-layouts  9 us

profile of v2, /device:TPU:1, one launch (start us, length us, event | category | flops | bytes accessed | tf_op | source)
XLA Modules:
  0.0 113.7 jit_solution(17400580506904883579)
XLA Ops:
  0.6 0.0 copy-start
  0.6 1.2 %copy-done = f32[1,1,512,512]{3,2,1,0:T(8,128)S(1)} copy-done((f32[1,1,512,512]{3,2,1,0:T(8,128)S(1)}, f32[1,1,512,512]{3,2,1,0:T(8,128)}, u32[]{:S(2)}) %copy-start) | copy-done | bytes 1048600
  1.9 0.0 copy-start.1
  1.9 1.2 %copy-done.1 = bf16[1,1,4,256,512]{4,3,2,1,0:T(8,128)(2,1)S(1)} copy-done((bf16[1,1,4,256,512]{4,3,2,1,0:T(8,128)(2,1)S(1)}, bf16[1,1,4,256,512]{4,3,2,1,0:T(8,128)(2,1)}, u32[]{:S(2)}) %copy-start.1) | copy-done | bytes 1048600
  3.1 0.0 copy-start.2
  3.1 1.0 copy-done.2
  4.1 0.0 copy-start.3
  4.1 0.7 copy-done.3
  4.8 104.1 %shard_map.86 = (f32[512,512]{1,0:T(8,128)S(1)}, f32[1536,512]{1,0:T(8,128)}) custom-call(f32[512,512]{1,0:T(8,128)S(1)} %bitcast.10, f32[4,256,512]{2,1,0:T(8,128)} %bitcast.15, bf16[4,256,512]{2,1,0:T(8,128)(2,1)S(1)} %bitcast.11, bf16[4,512,512]{2,1,0:T(8,128)(2,1)} %bitcast.16, s32[1,1024]{1,0:T(1,128)S(1)} %bitcast.13, bf16[1536,512]{1,0:T(8,128)(2,1)} %bitcast.17, ...), custom_call_target="tpu_custom_call" | custom-call | flops 8000000000 | bytes 12582912 | tf_op jit(solution)/shard_map/pallas_call | solution.py:261
  108.9 1.0 copy.11
  109.9 3.9 %copy.12 = f32[1,1,1536,512]{3,2,1,0:T(8,128)} copy(f32[1,1,1536,512]{3,2,1,0:T(8,128)} %bitcast.14) | data formatting | bytes 6291456
Async XLA Ops:
  0.6 1.2 %copy-start = (f32[1,1,512,512]{3,2,1,0:T(8,128)S(1)}, f32[1,1,512,512]{3,2,1,0:T(8,128)}, u32[]{:S(2)}) copy-start(f32[1,1,512,512]{3,2,1,0:T(8,128)} %param.7) | copy-start | bytes 3145732
  1.9 1.2 %copy-start.1 = (bf16[1,1,4,256,512]{4,3,2,1,0:T(8,128)(2,1)S(1)}, bf16[1,1,4,256,512]{4,3,2,1,0:T(8,128)(2,1)}, u32[]{:S(2)}) copy-start(bf16[1,1,4,256,512]{4,3,2,1,0:T(8,128)(2,1)} %param.9) | copy-start | bytes 3145732
  3.1 1.0 copy-start.2
  4.1 0.7 copy-start.3

commit v3 on v2

--- a/solution.py
+++ b/solution.py
@@ -28,19 +28,31 @@
     return joined(jnp.dot(left, right, preferred_element_type=F32))
 
 
-def dot_t(left, right):
-    return joined(
-        lax.dot_general(left, right, (((0,), (0,)), ((), ())), preferred_element_type=F32)
-    )
+PARTS = 4
+
+
+def hand_out(top_in, result_in, top_out, result_out, top_sem, result_sem):
+    copies = []
+    for source, target, sems in ((result_in, result_out, result_sem), (top_in, top_out, top_sem)):
+        rows = source.shape[0] // PARTS
+        for part in range(PARTS):
+            cut = pl.ds(part * rows, rows)
+            copies.append(pltpu.make_async_copy(source.at[cut], target.at[cut], sems.at[part]))
+    for copy in copies:
+        copy.start()
+    for copy in copies:
+        copy.wait()
 
 
 def kernel(
     owners, steps, chunks,
-    pivot_ref, sect_ref, y_ref, t_ref, route_ref, v_ref, f_ref,
+    pivot_hbm, sect_hbm, y_hbm, t_hbm, route_hbm, v_hbm, f_hbm,
+    top_hbm, out_hbm,
     top_ref, out_ref,
+    pivot_ref, sect_ref, y_ref, t_ref, route_ref, v_ref, f_ref, yt, tt,
     place, slot_row, pivots, pivots_out, contrib, send, arrived, arrived_cat,
     vt, ft, part, part_near, pair, pair_far, total,
-    chain_send, chain_recv, swap_send, swap_recv, sum_send, sum_recv,
+    load_sem, top_sem, out_sem, chain_send, chain_recv, swap_send, swap_recv, sum_send, sum_recv,
 ):
     front = lax.axis_index("front")
     me = lax.axis_index("sect")
@@ -50,7 +62,6 @@
     capacity = slots // owners
     depth = pivot_ref.shape[0]
     half = depth // 2
-    lag = steps // 2
     odd = lax.rem(me, 2)
     near = me + 1 - 2 * odd
     far = me + 2 - 4 * lax.rem(me // 2, 2)
@@ -64,6 +75,31 @@
             bit *= 2
         return found
 
+    def panel_of(step):
+        return lax.rem(me - step + steps, steps)
+
+    def panel_loads(step):
+        panel = panel_of(step)
+        pairs = ((sect_hbm, sect_ref), (y_hbm, y_ref), (t_hbm, t_ref))
+        return [
+            pltpu.make_async_copy(source.at[panel], target.at[panel], load_sem.at[3 * step + i])
+            for i, (source, target) in enumerate(pairs)
+        ]
+
+    def whole_load(index):
+        source, target = (
+            (pivot_hbm, pivot_ref), (route_hbm, route_ref), (v_hbm, v_ref), (f_hbm, f_ref)
+        )[index]
+        return pltpu.make_async_copy(source, target, load_sem.at[3 * steps + index])
+
+    for copy in [whole_load(0)] + panel_loads(0) + [whole_load(1)]:
+        copy.start()
+    for step in range(1, steps):
+        for copy in panel_loads(step):
+            copy.start()
+    whole_load(2).start()
+    whole_load(3).start()
+
     barrier = pltpu.get_barrier_semaphore()
 
     @pl.loop(1, owners)
@@ -75,31 +111,9 @@
             barrier, inc=1, device_id={"sect": lax.rem(me + shift, steps)}, device_id_type=MESH
         )
 
-    lanes = 128
-    before = (
-        lax.broadcasted_iota(jnp.int32, (lanes, lanes), 0)
-        <= lax.broadcasted_iota(jnp.int32, (lanes, lanes), 1)
-    ).astype(F32)
-    owner_ids = lax.broadcasted_iota(jnp.int32, (owners, lanes), 0)
-    carry = jnp.zeros((owners, 1), F32)
-    for group in range(row_count // lanes):
-        cut = slice(group * lanes, (group + 1) * lanes)
-        named = route_ref[:, cut]
-        hit = (owner_ids == named).astype(F32)
-        count = jnp.dot(hit, before, preferred_element_type=F32) + carry
-        rank = jnp.sum(hit * count, axis=0, keepdims=True) - 1.0
-        slot_row[:, cut] = named.astype(F32) * float(capacity) + rank
-        carry = carry + jnp.sum(hit, axis=1, keepdims=True)
-
-    @pl.loop(0, slots // TILE)
-    def _(tile):
-        ids = lax.broadcasted_iota(jnp.int32, (TILE, row_count), 0) + tile * TILE
-        hit = ids.astype(F32) == slot_row[...]
-        place[pl.ds(pl.multiple_of(tile * TILE, TILE), TILE), :] = hit.astype(F32).astype(BF16)
-
-    pl.semaphore_wait(barrier, owners - 1 + steps - 1)
-
     def columns(chunk):
+        if isinstance(chunk, int):
+            return pl.ds(chunk * WIDTH, WIDTH)
         return pl.ds(pl.multiple_of(chunk * WIDTH, WIDTH), WIDTH)
 
     def chain_copy(chunk, step):
@@ -123,20 +137,46 @@
             device_id_type=MESH,
         )
 
-    def reflect(chunk, step, pivot_block):
-        panel = lax.rem(me - step + steps, steps)
+    def build_place():
+        whole_load(1).wait()
+        lanes = 128
+        before = (
+            lax.broadcasted_iota(jnp.int32, (lanes, lanes), 0)
+            <= lax.broadcasted_iota(jnp.int32, (lanes, lanes), 1)
+        ).astype(F32)
+        owner_ids = lax.broadcasted_iota(jnp.int32, (owners, lanes), 0)
+        carry = jnp.zeros((owners, 1), F32)
+        for group in range(row_count // lanes):
+            cut = slice(group * lanes, (group + 1) * lanes)
+            named = route_ref[:, cut]
+            hit = (owner_ids == named).astype(F32)
+            count = jnp.dot(hit, before, preferred_element_type=F32) + carry
+            rank = jnp.sum(hit * count, axis=0, keepdims=True) - 1.0
+            slot_row[:, cut] = named.astype(F32) * float(capacity) + rank
+            carry = carry + jnp.sum(hit, axis=1, keepdims=True)
+
+        @pl.loop(0, slots // TILE)
+        def _(tile):
+            ids = lax.broadcasted_iota(jnp.int32, (TILE, row_count), 0) + tile * TILE
+            hit = ids.astype(F32) == slot_row[...]
+            place[pl.ds(pl.multiple_of(tile * TILE, TILE), TILE), :] = hit.astype(F32).astype(BF16)
+
+    def reflect(chunk, step):
+        panel = panel_of(step)
         row_block = sect_ref[panel, :, columns(chunk)]
-        vectors = y_ref[panel]
-        inner = pivot_block + dot_t(vectors, halves(row_block))
-        change = dot_t(t_ref[panel], halves(inner))
+        projected = dot(yt[panel], halves(row_block))
+        if step == 0:
+            pivot_block = pivot_ref[:, columns(chunk)]
+        else:
+            chain_copy(chunk, step - 1).wait_recv()
+            pivot_block = pivots[chunk * steps + step - 1]
+        change = dot(tt[panel], halves(pivot_block + projected))
         pivots_out[chunk * steps + step] = pivot_block - change
+        if step == 0 and isinstance(chunk, int):
+            pl.semaphore_wait(barrier, owners - 1 + steps - 1)
         chain_copy(chunk, step).start()
-        updated = row_block - dot(vectors, halves(change))
+        updated = row_block - dot(y_ref[panel], halves(change))
         contrib[chunk, pl.ds(pl.multiple_of(panel * rows, rows), rows), :] = halves(updated)
-
-    def later_step(chunk, step):
-        chain_copy(chunk, step - 1).wait_recv()
-        reflect(chunk, step, pivots[chunk * steps + step - 1])
 
     def exchange(chunk):
         @pl.loop(0, slots // TILE)
@@ -151,27 +191,26 @@
         own = pl.ds(pl.multiple_of(front * capacity, 8), capacity)
         arrived[chunk, own, :] = send[chunk, own, :]
 
-    @pl.loop(0, lag * (chunks + 1))
-    def _(slot):
-        within = lax.rem(slot, lag)
-
-        @pl.when(slot >= lag)
-        def _():
-            later_step(slot // lag - 1, within + lag)
-
-            @pl.when(within == lag - 1)
-            def _():
-                exchange(slot // lag - 1)
-
-        @pl.when(slot < lag * chunks)
-        def _():
-            @pl.when(within == 0)
-            def _():
-                reflect(slot // lag, 0, pivot_ref[:, columns(slot // lag)])
-
-            @pl.when(within > 0)
-            def _():
-                later_step(slot // lag, within)
+    whole_load(0).wait()
+    for step in range(steps):
+        for copy in panel_loads(step):
+            copy.wait()
+        panel = panel_of(step)
+        yt[panel] = y_ref[panel].T
+        tt[panel] = t_ref[panel].T
+        reflect(0, step)
+        if step == 0:
+            build_place()
+    exchange(0)
+
+    @pl.loop(1, chunks)
+    def _(chunk):
+        for step in range(steps):
+            reflect(chunk, step)
+        exchange(chunk)
+
+    whole_load(2).wait()
+    whole_load(3).wait()
 
     @pl.loop(0, slots // TILE)
     def _(tile):
@@ -184,6 +223,13 @@
     def _(chunk):
         chain_copy(chunk, steps - 1).wait_recv()
         top_ref[:, columns(chunk)] = pivots[chunk * steps + steps - 1]
+
+    top_copy = pltpu.make_async_copy(top_ref, top_hbm, top_sem)
+    top_copy.start()
+
+    def out_copy(chunk):
+        cut = columns(chunk)
+        return pltpu.make_async_copy(out_ref.at[:, cut], out_hbm.at[:, cut], out_sem.at[chunk])
 
     def sum_copy(chunk, stage, source, target, to):
         return pltpu.make_async_remote_copy(
@@ -236,15 +282,20 @@
             cut = pl.ds(pl.multiple_of(tile * TILE, TILE), TILE)
             out_ref[cut, columns(chunk)] = arrived[chunk, cut, :] - dot(v_ref[cut, :], change)
 
+        out_copy(chunk).start()
+
     @pl.loop(0, chunks)
     def _(chunk):
         for copy in sum_copies(chunk):
             copy.wait_send()
+        out_copy(chunk).wait()
         swapped(chunk, swap_send).wait()
 
     @pl.loop(0, chunks * steps)
     def _(index):
         chain_copy(index // steps, lax.rem(index, steps)).wait_send()
+
+    top_copy.wait()
 
 
 def local(pivot_rows, sections, sect_vectors, sect_factors, routes, parent_vectors, parent_factor):
@@ -256,7 +307,7 @@
     row_count = panels * rows
     chunks = columns // WIDTH
     half = depth // 2
-    vmem = pl.BlockSpec(memory_space=pltpu.VMEM)
+    hbm = pl.BlockSpec(memory_space=pltpu.HBM)
     dma = pltpu.SemaphoreType.DMA
     top, result = pl.pallas_call(
         functools.partial(kernel, owners, steps, chunks),
@@ -264,9 +315,20 @@
             jax.ShapeDtypeStruct((depth, columns), F32),
             jax.ShapeDtypeStruct((slots, columns), F32),
         ),
-        in_specs=[vmem] * 7,
-        out_specs=(vmem, vmem),
+        in_specs=[hbm] * 7,
+        out_specs=(hbm, hbm),
         scratch_shapes=[
+            pltpu.VMEM((depth, columns), F32),
+            pltpu.VMEM((slots, columns), F32),
+            pltpu.VMEM((depth, columns), F32),
+            pltpu.VMEM((panels, rows, columns), F32),
+            pltpu.VMEM((panels, rows, depth), BF16),
+            pltpu.VMEM((panels, depth, depth), BF16),
+            pltpu.VMEM((1, row_count), jnp.int32),
+            pltpu.VMEM((slots, depth), BF16),
+            pltpu.VMEM((depth, depth), BF16),
+            pltpu.VMEM((panels, depth, rows), BF16),
+            pltpu.VMEM((panels, depth, depth), BF16),
             pltpu.VMEM((slots, row_count), BF16),
             pltpu.VMEM((1, row_count), F32),
             pltpu.VMEM((chunks * steps, depth, WIDTH), F32),
@@ -282,6 +344,9 @@
             pltpu.VMEM((chunks, half, WIDTH), F32),
             pltpu.VMEM((chunks, half, WIDTH), F32),
             pltpu.VMEM((chunks, depth, WIDTH), F32),
+            dma((3 * steps + 4,)),
+            dma,
+            dma((chunks,)),
             dma((chunks * steps,)),
             dma((chunks * steps,)),
             dma((chunks,)),
@@ -290,7 +355,7 @@
             dma((chunks * 3,)),
         ],
         compiler_params=pltpu.CompilerParams(
-            collective_id=0, has_side_effects=True, vmem_limit_bytes=50 * 2**20
+            collective_id=0, has_side_effects=True, vmem_limit_bytes=62 * 2**20
         ),
         cost_estimate=pl.CostEstimate(
             flops=8 * 10**9, bytes_accessed=12 * 2**20, transcendentals=0
@@ -304,6 +369,18 @@
         parent_vectors[0, 0],
         parent_factor[0],
     )
+    top, result = pl.pallas_call(
+        hand_out,
+        out_shape=(
+            jax.ShapeDtypeStruct((depth, columns), F32),
+            jax.ShapeDtypeStruct((slots, columns), F32),
+        ),
+        in_specs=[hbm] * 2,
+        out_specs=(hbm, hbm),
+        scratch_shapes=[dma((PARTS,)), dma((PARTS,))],
+        compiler_params=pltpu.CompilerParams(vmem_limit_bytes=62 * 2**20),
+        cost_estimate=pl.CostEstimate(flops=0, bytes_accessed=8 * 2**20, transcendentals=0),
+    )(top, result)
     return (top[None, None], result[None, None])
 
 

time: 114 us -> 230 us (2.02)
  Pallas kernels: 104 us -> 229 us
  local copies, waits for them, and re-layouts: 9 us -> 0 us
    pallas_call x0 -> x1, Pallas kernels: none -> 128 us  [local(): pl.pallas_call(hand_out, out_shape=(jax.ShapeDtypeStruct((depth, columns)...]
    unnamed x10 -> x0, local copies, waits for them, and re-layouts: 9 us -> none
    pallas_call x1, Pallas kernels: 104 us -> 101 us  [local(): pl.pallas_call(functools.partial(kernel, owners, steps, chunks), out_shap...]
where the time goes in v3:
time: 230 us; the launch traced here: 229 us
  Pallas kernels  229 us (100%)
    pallas_call x1, Pallas kernels, local(): pl.pallas_call(hand_out, out_shape=(jax.ShapeDtypeStruct((depth, columns)...  128 us
    pallas_call x1, Pallas kernels, local(): pl.pallas_call(functools.partial(kernel, owners, steps, chunks), out_shap...  101 us

profile of v3, /device:TPU:1, one launch (start us, length us, event | category | flops | bytes accessed | tf_op | source)
XLA Modules:
  0.0 229.4 jit_solution(3669060309344581398)
XLA Ops:
  0.6 100.6 %shard_map.86 = (f32[512,512]{1,0:T(8,128)}, f32[1536,512]{1,0:T(8,128)}) custom-call(f32[512,512]{1,0:T(8,128)} %bitcast.13, f32[4,256,512]{2,1,0:T(8,128)} %bitcast.10, bf16[4,256,512]{2,1,0:T(8,128)(2,1)} %bitcast.14, bf16[4,512,512]{2,1,0:T(8,128)(2,1)} %bitcast.11, s32[1,1024]{1,0:T(1,128)} %bitcast.17, bf16[1536,512]{1,0:T(8,128)(2,1)} %bitcast.12, ...), custom_call_target="tpu_custom_call" | custom-call | flops 8000000000 | bytes 12582912 | tf_op jit(solution)/shard_map/pallas_call | solution.py:312
  101.2 128.2 %shard_map.87 = (f32[512,512]{1,0:T(8,128)}, f32[1536,512]{1,0:T(8,128)}) custom-call(f32[512,512]{1,0:T(8,128)} %get-tuple-element.6.top_in, f32[1536,512]{1,0:T(8,128)} %get-tuple-element.7.result_in), custom_call_target="tpu_custom_call" | custom-call | bytes 8388608 | tf_op jit(solution)/shard_map/pallas_call | solution.py:372

commit v4 on v3

--- a/solution.py
+++ b/solution.py
@@ -31,17 +31,24 @@
 PARTS = 4
 
 
-def hand_out(top_in, result_in, top_out, result_out, top_sem, result_sem):
-    copies = []
-    for source, target, sems in ((result_in, result_out, result_sem), (top_in, top_out, top_sem)):
+def hand_out(top_in, result_in, top_out, result_out, top_mid, result_mid, in_sem, out_sem):
+    loads, stores = [], []
+    for source, held, target in (
+        (result_in, result_mid, result_out), (top_in, top_mid, top_out)
+    ):
         rows = source.shape[0] // PARTS
         for part in range(PARTS):
             cut = pl.ds(part * rows, rows)
-            copies.append(pltpu.make_async_copy(source.at[cut], target.at[cut], sems.at[part]))
-    for copy in copies:
-        copy.start()
-    for copy in copies:
-        copy.wait()
+            index = len(loads)
+            loads.append(pltpu.make_async_copy(source.at[cut], held.at[cut], in_sem.at[index]))
+            stores.append(pltpu.make_async_copy(held.at[cut], target.at[cut], out_sem.at[index]))
+    for load in loads:
+        load.start()
+    for load, store in zip(loads, stores):
+        load.wait()
+        store.start()
+    for store in stores:
+        store.wait()
 
 
 def kernel(
@@ -172,7 +179,7 @@
             pivot_block = pivots[chunk * steps + step - 1]
         change = dot(tt[panel], halves(pivot_block + projected))
         pivots_out[chunk * steps + step] = pivot_block - change
-        if step == 0 and isinstance(chunk, int):
+        if step == 0 and isinstance(chunk, int) and chunk == 0:
             pl.semaphore_wait(barrier, owners - 1 + steps - 1)
         chain_copy(chunk, step).start()
         updated = row_block - dot(y_ref[panel], halves(change))
@@ -184,9 +191,10 @@
             cut = pl.ds(pl.multiple_of(tile * TILE, TILE), TILE)
             send[chunk, cut, :] = dot(place[cut, :], contrib[chunk])
 
-        @pl.loop(1, owners)
-        def _(m):
-            swap_copy(chunk, owners - m).start()
+        @pl.loop(0, owners - 1)
+        def _(turn):
+            m = 1 + lax.rem((owners // 2 - 1) * (turn + 1) + 2 * odd, owners - 1)
+            swap_copy(chunk, m).start()
 
         own = pl.ds(pl.multiple_of(front * capacity, 8), capacity)
         arrived[chunk, own, :] = send[chunk, own, :]
@@ -198,6 +206,8 @@
         panel = panel_of(step)
         yt[panel] = y_ref[panel].T
         tt[panel] = t_ref[panel].T
+        if step == steps - 1 and chunks > 1:
+            reflect(1, 0)
         reflect(0, step)
         if step == 0:
             build_place()
@@ -205,8 +215,14 @@
 
     @pl.loop(1, chunks)
     def _(chunk):
-        for step in range(steps):
+        for step in range(1, steps - 1):
             reflect(chunk, step)
+
+        @pl.when(chunk + 1 < chunks)
+        def _():
+            reflect(chunk + 1, 0)
+
+        reflect(chunk, steps - 1)
         exchange(chunk)
 
     whole_load(2).wait()
@@ -377,7 +393,12 @@
         ),
         in_specs=[hbm] * 2,
         out_specs=(hbm, hbm),
-        scratch_shapes=[dma((PARTS,)), dma((PARTS,))],
+        scratch_shapes=[
+            pltpu.VMEM((depth, columns), F32),
+            pltpu.VMEM((slots, columns), F32),
+            dma((2 * PARTS,)),
+            dma((2 * PARTS,)),
+        ],
         compiler_params=pltpu.CompilerParams(vmem_limit_bytes=62 * 2**20),
         cost_estimate=pl.CostEstimate(flops=0, bytes_accessed=8 * 2**20, transcendentals=0),
     )(top, result)

time: 230 us -> 106 us (0.46)
  Pallas kernels: 229 us -> 105 us
    pallas_call x1, Pallas kernels: 128 us -> 3.27 us  [local(): pl.pallas_call(hand_out, out_shape=(jax.ShapeDtypeStruct((depth, columns)...]
where the time goes in v4:
time: 106 us
  Pallas kernels  105 us (99%)
    pallas_call x1, Pallas kernels, local(): pl.pallas_call(functools.partial(kernel, owners, steps, chunks), out_shap...  102 us
    pallas_call x1, Pallas kernels, local(): pl.pallas_call(hand_out, out_shape=(jax.ShapeDtypeStruct((depth, columns)...  3.27 us

profile of v4, /device:TPU:1, one launch (start us, length us, event | category | flops | bytes accessed | tf_op | source)
XLA Modules:
  0.0 106.1 jit_solution(4226714092498593777)
XLA Ops:
  0.6 102.2 %shard_map.86 = (f32[512,512]{1,0:T(8,128)}, f32[1536,512]{1,0:T(8,128)}) custom-call(f32[512,512]{1,0:T(8,128)} %bitcast.13, f32[4,256,512]{2,1,0:T(8,128)} %bitcast.10, bf16[4,256,512]{2,1,0:T(8,128)(2,1)} %bitcast.14, bf16[4,512,512]{2,1,0:T(8,128)(2,1)} %bitcast.11, s32[1,1024]{1,0:T(1,128)} %bitcast.17, bf16[1536,512]{1,0:T(8,128)(2,1)} %bitcast.12, ...), custom_call_target="tpu_custom_call" | custom-call | flops 8000000000 | bytes 12582912 | tf_op jit(solution)/shard_map/pallas_call | solution.py:328
  102.8 3.3 %shard_map.87 = (f32[512,512]{1,0:T(8,128)}, f32[1536,512]{1,0:T(8,128)}) custom-call(f32[512,512]{1,0:T(8,128)} %get-tuple-element.6.top_in, f32[1536,512]{1,0:T(8,128)} %get-tuple-element.7.result_in), custom_call_target="tpu_custom_call" | custom-call | bytes 8388608 | tf_op jit(solution)/shard_map/pallas_call | solution.py:388

commit v5 on v4

--- a/solution.py
+++ b/solution.py
@@ -73,6 +73,7 @@
     near = me + 1 - 2 * odd
     far = me + 2 - 4 * lax.rem(me // 2, 2)
     right = lax.rem(me + 1, steps)
+    middle = lax.rem(front // (owners // 2) + front // (owners // 4), 2)
 
     def peer(m):
         found = 0
@@ -191,9 +192,12 @@
             cut = pl.ds(pl.multiple_of(tile * TILE, TILE), TILE)
             send[chunk, cut, :] = dot(place[cut, :], contrib[chunk])
 
-        @pl.loop(0, owners - 1)
+        @pl.loop(1, owners)
         def _(turn):
-            m = 1 + lax.rem((owners // 2 - 1) * (turn + 1) + 2 * odd, owners - 1)
+            i = owners - turn
+            upper = i // (owners // 2)
+            lower = lax.rem(i // (owners // 4), 2) * (1 - upper)
+            m = i + middle * ((owners // 2) * lower - (owners // 4) * upper)
             swap_copy(chunk, m).start()
 
         own = pl.ds(pl.multiple_of(front * capacity, 8), capacity)

time: 106 us -> 102 us (0.962)
  the two profiles are of different devices: /device:TPU:1 before, /device:TPU:19 now
where the time goes in v5:
time: 102 us
  Pallas kernels  102 us (100%)
    pallas_call x1, Pallas kernels, local(): pl.pallas_call(functools.partial(kernel, owners, steps, chunks), out_shap...  98.4 us
    pallas_call x1, Pallas kernels, local(): pl.pallas_call(hand_out, out_shape=(jax.ShapeDtypeStruct((depth, columns)...  3.27 us

profile of v5, /device:TPU:19, one launch (start us, length us, event | category | flops | bytes accessed | tf_op | source)
XLA Modules:
  0.0 102.3 jit_solution(9743007176564286839)
XLA Ops:
  0.6 98.4 %shard_map.86 = (f32[512,512]{1,0:T(8,128)}, f32[1536,512]{1,0:T(8,128)}) custom-call(f32[512,512]{1,0:T(8,128)} %bitcast.13, f32[4,256,512]{2,1,0:T(8,128)} %bitcast.10, bf16[4,256,512]{2,1,0:T(8,128)(2,1)} %bitcast.14, bf16[4,512,512]{2,1,0:T(8,128)(2,1)} %bitcast.11, s32[1,1024]{1,0:T(1,128)} %bitcast.17, bf16[1536,512]{1,0:T(8,128)(2,1)} %bitcast.12, ...), custom_call_target="tpu_custom_call" | custom-call | flops 8000000000 | bytes 12582912 | tf_op jit(solution)/shard_map/pallas_call | solution.py:332
  99.0 3.3 %shard_map.87 = (f32[512,512]{1,0:T(8,128)}, f32[1536,512]{1,0:T(8,128)}) custom-call(f32[512,512]{1,0:T(8,128)} %get-tuple-element.6.top_in, f32[1536,512]{1,0:T(8,128)} %get-tuple-element.7.result_in), custom_call_target="tpu_custom_call" | custom-call | bytes 8388608 | tf_op jit(solution)/shard_map/pallas_call | solution.py:392
